TPU v7x, 128 devices: a whole 4x4x4 slice. The times are simulated.
128 devices in a mesh: slab: 16 (over x, y), span: 8 (over z, core).
Axes of the slice: x: 4, y: 4, z: 4, core: 2. Of those that a mesh axis runs over, the one named last changes fastest.
Arguments:
- velocity: float32 [3, 128, 256, 512], P(None, 'slab', 'span'), may hold values from -6 to 6
- profile: float32 [32, 3, 262144], P(None, None, ('slab', 'span')), may hold values from -3 to 3
- normal: float32 [3, 262144], P(None, ('slab', 'span')), may hold values from -1 to 1, as said below
- height: float32 [262144], P(('slab', 'span')), may hold values from 0.5 to 2
- pressure_grad: float32 [3, 262144], P(None, ('slab', 'span')), may hold values from -8 to 8
- owner_device: int32 [262144, 1], P(('slab', 'span')), may hold values from 0 to 127; in each aligned block of 2048 rows (0 to 2047, 2048 to 4095, ...) at most 32 rows name the same one
- match_cell: int32 [262144], P(('slab', 'span')), may hold values from 0 to 131071
Outputs:
- new_velocity: float32 [3, 128, 256, 512], P(None, 'slab', 'span')
- wall_profile: float32 [32, 3, 262144], P(None, None, ('slab', 'span'))
- wall_stress: float32 [3, 262144], P(None, ('slab', 'span'))
Inputs may be any that keep to these rules, and one draw needn't show every extreme that they name: `owner_device`: among the 2048 hull cells of one device (aligned blocks of rows), at most 32 have their matching cell on any one device, and exactly 32 on some device. `match_cell`: A local index (x * 32 + y) * 512 + z within the owner's block of the volume. `normal`: each column is a unit vector with vertical component between -0.9 and 0.9.
All inputs are finite; a program needn't handle non-finite values.
Results may differ from a plain program's by a relative error of at most 0.0003.
Values sent between devices are 32-bit elements; how exact they have to be, the bound alone decides.
A program may use at most 192 MiB of HBM per device.

v0:
```python
import jax
import jax.numpy as jnp
from jax import lax
from jax.sharding import PartitionSpec as P

TILE = 128
PICARD = 2


time_step = 0.1
viscosity = 0.001
smag_coef = 0.02
kappa_coef = 0.41
damping_plus = 26.0
stretch = 1.12
area_ratio = 4.0
third_part = 1.0 / 3.0
two_thirds = 2.0 / 3.0


def extended(array, sides, width):
    for axis, dim in sides:
        devices, length = (lax.axis_size(axis), array.shape[dim])
        up = [(i, (i + 1) % devices) for i in range(devices - 1)]
        down = [(j, i) for i, j in up]
        last = lax.slice_in_dim(array, length - width, length, axis=dim)
        leading = lax.slice_in_dim(array, 0, width, axis=dim)
        before = lax.ppermute(last, axis, up)
        after = lax.ppermute(leading, axis, down)
        array = jnp.concatenate([before, array, after], axis=dim)
    return array


def shift_depth(block, forward):
    border = jnp.zeros_like(block[..., :1])
    if forward:
        return jnp.concatenate([block[..., 1:], border], axis=-1)
    return jnp.concatenate([border, block[..., :-1]], axis=-1)


def rhs_core(padded):
    center = padded[:, 1:-1, 1:-1, :]
    x_plus = padded[:, 2:, 1:-1, :]
    x_minus = padded[:, :-2, 1:-1, :]
    y_plus = padded[:, 1:-1, 2:, :]
    y_minus = padded[:, 1:-1, :-2, :]
    z_plus = shift_depth(center, True)
    z_minus = shift_depth(center, False)
    grad_x = 0.5 * (x_plus - x_minus)
    grad_y = 0.5 * (y_plus - y_minus)
    grad_z = 0.5 * (z_plus - z_minus)
    laplace = x_plus + x_minus + y_plus + y_minus + z_plus + z_minus - 6.0 * center
    shear = jnp.sqrt(jnp.sum(grad_x * grad_x + grad_y * grad_y + grad_z * grad_z, axis=0))
    eddy_visc = viscosity + smag_coef * shear
    advect = center[0:1] * grad_x + center[1:2] * grad_y + center[2:3] * grad_z
    return eddy_visc[None] * laplace - advect


def thomas(sub_diag, main_diag, super_diag, right_side):
    points = right_side.shape[0]
    reduced_c = []
    reduced_d = []
    prev_c = jnp.zeros_like(main_diag[0])
    prev_d = jnp.zeros_like(right_side[0])
    for level in range(points):
        divisor = main_diag[level] - sub_diag[level] * prev_c
        prev_c = super_diag[level] / divisor
        prev_d = (right_side[level] - sub_diag[level][None] * prev_d) / divisor[None]
        reduced_c.append(prev_c)
        reduced_d.append(prev_d)
    values = [None] * points
    following = jnp.zeros_like(right_side[0])
    for level in range(points - 1, -1, -1):
        following = reduced_d[level] - reduced_c[level][None] * following
        values[level] = following
    return jnp.stack(values)


def tangential(vector, normal):
    return vector - jnp.sum(vector * normal, axis=0, keepdims=True) * normal


def wall_model(profile, matched, normal, height, pressure_grad):
    points = profile.shape[0]
    levels = jnp.arange(points + 2, dtype=jnp.float32)
    fraction = (stretch**levels - 1.0) / (stretch ** (points + 1) - 1.0)
    heights = fraction[:, None] * height[None, :]
    target = tangential(matched, normal)
    forcing = tangential(pressure_grad, normal)
    spacing = heights[1:] - heights[:-1]
    face_height = 0.5 * (heights[1:] + heights[:-1])
    cell_span = 0.5 * (heights[2:] - heights[:-2])
    first_height = heights[1]
    current = profile
    for sweep in range(PICARD):
        stress = viscosity * current[0] / first_height[None]
        speed = jnp.sqrt(jnp.sqrt(jnp.sum(stress * stress, axis=0)))
        damping = 1.0 - jnp.exp(-face_height * speed[None] / (viscosity * damping_plus))
        diffusivity = viscosity + kappa_coef * face_height * speed[None] * damping * damping
        conductance = diffusivity / spacing
        lower_w = conductance[:-1] / cell_span
        upper_w = conductance[1:] / cell_span
        sub_diag = -time_step * lower_w
        super_diag = -time_step * upper_w
        main_diag = 1.0 + time_step * (lower_w + upper_w)
        right_side = profile - time_step * forcing[None]
        right_side = right_side.at[-1].add(time_step * upper_w[-1][None] * target)
        current = thomas(sub_diag, main_diag, super_diag, right_side)
    stress = viscosity * current[0] / first_height[None]
    return (current, stress)


def section_rhs(field):
    padded = extended(field, (("slab", 1), ("span", 2)), 1)
    return rhs_core(padded)


def outer_step(velocity):
    section_one = velocity + time_step * section_rhs(velocity)
    section_two = 0.75 * velocity + 0.25 * (section_one + time_step * section_rhs(section_one))
    return third_part * velocity + two_thirds * (section_two + time_step * section_rhs(section_two))


def per_device(velocity, profile, normal, height, pressure_grad, owner_device, match_cell):
    slab_count = lax.axis_size("slab")
    span_count = lax.axis_size("span")
    devices = slab_count * span_count
    hull_count = owner_device.shape[0]
    slot_count = 2 * hull_count // devices
    tile_count = hull_count // TILE
    target = owner_device[:, 0]
    is_owner = target[:, None] == jnp.arange(devices, dtype=jnp.int32)[None, :]
    onehot = is_owner.astype(jnp.bfloat16).reshape(tile_count, TILE, devices)
    before = (jnp.arange(TILE)[:, None] > jnp.arange(TILE)[None, :]).astype(jnp.bfloat16)
    within = jnp.einsum("ij,tjd->tid", before, onehot, preferred_element_type=jnp.float32)
    totals = jnp.sum(onehot, axis=1, dtype=jnp.float32)
    offsets = jnp.cumsum(totals, axis=0) - totals
    ranks_all = (within + offsets[:, None, :]).reshape(hull_count, devices)
    slot_rank = jnp.sum(jnp.where(is_owner, ranks_all, 0.0), axis=1).astype(jnp.int32)
    slot_index = target * slot_count + slot_rank
    request = (
        jnp.zeros((devices * slot_count,), jnp.int32)
        .at[slot_index]
        .set(match_cell)
        .reshape(devices, 1, slot_count)
    )
    cell_rows = velocity.reshape(3, -1).T
    indices = lax.all_to_all(request, ("slab", "span"), split_axis=0, concat_axis=0, tiled=True)
    wanted = indices[:, 0, :]
    taken = jnp.transpose(cell_rows[wanted], (0, 2, 1))
    replies = lax.all_to_all(taken, ("slab", "span"), split_axis=0, concat_axis=0, tiled=True)
    reply_rows = jnp.transpose(replies, (0, 2, 1)).reshape(devices * slot_count, 3)
    matched = reply_rows[slot_index].T
    wall_profile, wall_stress = wall_model(profile, matched, normal, height, pressure_grad)
    push = -time_step * area_ratio * wall_stress
    slot_rows = jnp.zeros((devices * slot_count, 3), jnp.float32).at[slot_index].set(push.T)
    returned = jnp.transpose(slot_rows.reshape(devices, slot_count, 3), (0, 2, 1))
    stepped = outer_step(velocity)
    arrived = lax.all_to_all(returned, ("slab", "span"), split_axis=0, concat_axis=0, tiled=True)
    cell_index = indices[:, 0, :].reshape(-1)
    arrived_rows = jnp.transpose(arrived, (0, 2, 1)).reshape(devices * slot_count, 3)
    step_rows = stepped.reshape(3, -1).T.at[cell_index].add(arrived_rows)
    new_velocity = step_rows.T.reshape(stepped.shape)
    return (new_velocity, wall_profile, wall_stress)


def solution(mesh):
    return jax.shard_map(
        per_device,
        mesh=mesh,
        in_specs=(
            P(None, "slab", "span", None),
            P(None, None, ("slab", "span")),
            P(None, ("slab", "span")),
            P(("slab", "span")),
            P(None, ("slab", "span")),
            P(("slab", "span"), None),
            P(("slab", "span")),
        ),
        out_specs=(
            P(None, "slab", "span", None),
            P(None, None, ("slab", "span")),
            P(None, ("slab", "span")),
        ),
        check_vma=False,
    )
```

profile of v0, /device:TPU:13, one launch (start us, length us, event | category | flops | bytes accessed | tf_op | source)
XLA Modules:
  0.0 941.7 jit_solution(16449766601740064268)
XLA Ops:
  0.7 1.0 convert_reduce_fusion
  1.7 1.2 fusion.2
  3.0 8.2 scatter_custom_fusion
  11.9 10.7 %all-to-all-start = ((s32[128,1,32]{2,1,0:T(1,128)}), s32[128,1,32]{2,1,0:T(1,128)S(1)}, u32[]{:S(2)}, u32[]{:S(2)}) async-start(s32[128,1,32]{2,1,0:T(1,128)} %bitcast.16), calls=%async_computation | async-start | bytes 131072 | tf_op jit(solution)/shard_map/all_to_all | solution.py:148
  22.6 0.8 fusion.104
  23.4 3.1 collective-permute-start.1
  26.5 2.2 collective-permute-start
  28.8 1.7 fusion.105
  30.6 1.2 multiply_bitcast_fusion.2
  31.8 32.6 %copy.130 = f32[3,8,32,512]{0,3,2,1:T(8,128)} copy(f32[3,8,32,512]{3,2,1,0:T(8,128)S(1)} %copy-done) | data formatting | bytes 3145728 | tf_op args[0]
  65.1 1.5 reshape.15657
  66.6 0.7 broadcast_clamp_fusion
  67.3 146.2 %gather_fusion = f32[4096,3]{1,0:T(8,128)} fusion(f32[131072,3]{1,0:T(8,128)} %bitcast.146, s32[4096]{0:T(1024)S(1)} %broadcast_clamp_fusion), kind=kCustom, calls=%fused_computation | custom fusion | bytes 114688 | tf_op jit(solution)/shard_map/gather | solution.py:150
  213.5 3.1 copy.131
  216.6 9.8 %all-to-all-start.1 = ((f32[128,3,32]{2,1,0:T(4,128)}), f32[128,3,32]{2,1,0:T(4,128)}, u32[]{:S(2)}, u32[]{:S(2)}) async-start(f32[128,3,32]{2,1,0:T(4,128)} %bitcast.733), calls=%async_computation.1 | async-start | bytes 524288 | tf_op jit(solution)/shard_map/all_to_all | solution.py:151
  227.5 1.4 reduce.8
  228.9 1.5 reshape_squeeze.3
  230.4 3.9 all-to-all-done.1
  234.3 3.1 copy.132
  237.5 9.1 gather_fusion.1
  246.6 1.6 copy.133
  248.1 0.8 fusion.29
  249.0 0.8 subtract_multiply_fusion
  249.7 1.8 broadcast_subtract_fusion
  252.2 0.8 fusion.96
  253.1 0.8 fusion.93
  254.4 0.8 fusion.97
  255.8 1.5 multiply_subtract_fusion
  257.3 1.6 multiply_bitcast_fusion.3
  258.9 1.3 copy.134
  260.2 7.4 scatter_custom_fusion.1
  267.6 3.1 copy.135
  270.7 7.2 all-to-all-start.2
  277.9 1.6 constant_dynamic-update-slice_fusion.2
  279.7 1.4 constant_dynamic-update-slice_fusion.1
  281.2 1.7 constant_dynamic-update-slice_fusion
  282.9 1.9 fusion.99
  284.9 3.5 collective-permute-start.3
  288.4 2.1 collective-permute-start.2
  310.7 7.2 stack.2
  317.9 2.2 copy.171
  320.2 4.0 add_reduce_fusion.2
  324.4 3.6 multiply_add_fusion.2
  328.0 3.2 collective-permute-start.5
  331.1 2.1 collective-permute-start.4
  333.9 1.6 collective-permute-done.5
  335.5 3.1 collective-permute-done.4
  338.7 5.0 collective-permute-start.7
  343.7 1.9 collective-permute-start.6
  345.9 3.4 collective-permute-done.6
  349.3 1.7 add_reduce_fusion.1
  351.1 2.3 multiply_add_fusion.1
  353.5 2.9 collective-permute-start.9
  356.3 2.4 collective-permute-start.8
  359.4 0.7 collective-permute-done.9
  360.1 4.2 collective-permute-done.8
  364.4 4.4 collective-permute-start.11
  368.8 2.2 collective-permute-start.10
  371.2 3.1 collective-permute-done.10
  374.3 1.7 add_reduce_fusion
  376.2 2.3 multiply_add_fusion
  378.5 32.6 %copy.126 = f32[3,8,32,512]{0,3,2,1:T(8,128)} copy(f32[3,8,32,512]{3,2,1,0:T(8,128)S(1)} %multiply_add_fusion) | data formatting | bytes 3145728 | tf_op jit(solution)/shard_map/add | solution.py:121
  411.2 491.3 %scatter_fusion = f32[131072,3]{1,0:T(8,128)} fusion(f32[131072,3]{1,0:T(8,128)} %bitcast.10, s32[4096]{0:T(1024)S(1)} %bitcast.960, f32[4096,3]{1,0:T(8,128)} %bitcast.728), kind=kCustom, calls=%fused_computation.4 | custom fusion | flops 12288 | bytes 163840 | tf_op jit(solution)/shard_map/scatter-add | solution.py:162
  902.5 39.2 %copy.170 = f32[3,8,32,512]{3,2,1,0:T(8,128)} copy(f32[3,8,32,512]{0,3,2,1:T(8,128)} %bitcast.263) | data formatting | bytes 3145728
  (167 shorter events, 26.9 us)
Async XLA Ops:
  0.6 2.3 copy-start.39
  0.6 22.0 %copy-start = (f32[3,8,32,512]{3,2,1,0:T(8,128)S(1)}, f32[3,8,32,512]{3,2,1,0:T(8,128)}, u32[]{:S(2)}) copy-start(f32[3,8,32,512]{3,2,1,0:T(8,128)} %param.11) | copy-start | bytes 4718596
  3.0 25.8 %copy-start.40 = (s32[2048,1]{0,1:T(1,128)}, s32[2048,1]{0,1:T(1,128)S(1)}, u32[]{:S(2)}) copy-start(s32[2048,1]{0,1:T(1,128)S(1)} %compare_select_fusion.2) | copy-start | bytes 24580
  11.9 52.5 %all-to-all-start = ((s32[128,1,32]{2,1,0:T(1,128)}), s32[128,1,32]{2,1,0:T(1,128)S(1)}, u32[]{:S(2)}, u32[]{:S(2)}) async-start(s32[128,1,32]{2,1,0:T(1,128)} %bitcast.16), calls=%async_computation | async-start | bytes 131072 | tf_op jit(solution)/shard_map/all_to_all | solution.py:148
  23.4 254.5 %collective-permute-start.1 = (f32[3,1,32,512]{3,2,1,0:T(8,128)}, f32[3,1,32,512]{3,2,1,0:T(8,128)}, u32[]{:S(2)}, u32[]{:S(2)}) collective-permute-start(f32[3,1,32,512]{3,2,1,0:T(8,128)} %get-tuple-element.250), channel_id=1, source_target_pairs={{0,8},{8,16},{16,24},{24,32},{32,40},{40,48},{48,56},{56,64},{64,7... | collective-permute-start | bytes 589832 | tf_op jit(solution)/shard_map/ppermute | solution.py:28
  26.5 254.7 %collective-permute-start = (f32[3,1,32,512]{3,2,1,0:T(8,128)}, f32[3,1,32,512]{3,2,1,0:T(8,128)}, u32[]{:S(2)}, u32[]{:S(2)}) collective-permute-start(f32[3,1,32,512]{3,2,1,0:T(8,128)} %get-tuple-element.251), channel_id=1, source_target_pairs={{8,0},{16,8},{24,16},{32,24},{40,32},{48,40},{56,48},{64,56},{72,6... | collective-permute-start | bytes 589832 | tf_op jit(solution)/shard_map/ppermute | solution.py:29
  28.7 1.7 copy-start.43
  213.5 12.9 %copy-start.41 = (s32[2048,1]{0,1:T(1,128)S(1)}, s32[2048,1]{0,1:T(1,128)}, u32[]{:S(2)}) copy-start(s32[2048,1]{0,1:T(1,128)} %copy-done.40) | copy-start | bytes 24580
  216.6 17.8 %all-to-all-start.1 = ((f32[128,3,32]{2,1,0:T(4,128)}), f32[128,3,32]{2,1,0:T(4,128)}, u32[]{:S(2)}, u32[]{:S(2)}) async-start(f32[128,3,32]{2,1,0:T(4,128)} %bitcast.733), calls=%async_computation.1 | async-start | bytes 524288 | tf_op jit(solution)/shard_map/all_to_all | solution.py:151
  228.9 8.6 copy-start.42
  237.5 10.7 %copy-start.5 = (f32[3,2048]{1,0:T(4,128)S(1)}, f32[3,2048]{1,0:T(4,128)}, u32[]{:S(2)}) copy-start(f32[3,2048]{1,0:T(4,128)} %param.13) | copy-start | bytes 73732
  270.7 47.2 %all-to-all-start.2 = ((f32[128,3,32]{2,1,0:T(4,128)}), f32[128,3,32]{2,1,0:T(4,128)S(1)}, u32[]{:S(2)}, u32[]{:S(2)}) async-start(f32[128,3,32]{2,1,0:T(4,128)} %bitcast.732), calls=%async_computation.2 | async-start | bytes 524288 | tf_op jit(solution)/shard_map/all_to_all | solution.py:159
  279.5 11.0 %copy-start.38 = (s32[4096,1]{0,1:T(1,128)S(1)}, s32[4096,1]{0,1:T(1,128)}, u32[]{:S(2)}) copy-start(s32[4096,1]{0,1:T(1,128)} %reshape_squeeze.3) | copy-start | bytes 49156
  279.5 11.1 %copy-start.37 = (f32[1,3,2048]{2,1,0:T(4,128)S(1)}, f32[1,3,2048]{2,1,0:T(4,128)}, u32[]{:S(2)}) copy-start(f32[1,3,2048]{2,1,0:T(4,128)} %get-tuple-element.44) | copy-start | bytes 73732
  279.5 11.7 %copy-start.36 = (f32[1,3,2048]{2,1,0:T(4,128)S(1)}, f32[1,3,2048]{2,1,0:T(4,128)}, u32[]{:S(2)}) copy-start(f32[1,3,2048]{2,1,0:T(4,128)} %get-tuple-element.45) | copy-start | bytes 73732
  279.5 12.3 %copy-start.35 = (f32[1,3,2048]{2,1,0:T(4,128)S(1)}, f32[1,3,2048]{2,1,0:T(4,128)}, u32[]{:S(2)}) copy-start(f32[1,3,2048]{2,1,0:T(4,128)} %get-tuple-element.46) | copy-start | bytes 73732
  279.5 13.0 %copy-start.34 = (f32[1,3,2048]{2,1,0:T(4,128)S(1)}, f32[1,3,2048]{2,1,0:T(4,128)}, u32[]{:S(2)}) copy-start(f32[1,3,2048]{2,1,0:T(4,128)} %get-tuple-element.47) | copy-start | bytes 73732
  279.6 13.6 %copy-start.33 = (f32[1,3,2048]{2,1,0:T(4,128)S(1)}, f32[1,3,2048]{2,1,0:T(4,128)}, u32[]{:S(2)}) copy-start(f32[1,3,2048]{2,1,0:T(4,128)} %get-tuple-element.48) | copy-start | bytes 73732
  279.6 14.2 %copy-start.32 = (f32[1,3,2048]{2,1,0:T(4,128)S(1)}, f32[1,3,2048]{2,1,0:T(4,128)}, u32[]{:S(2)}) copy-start(f32[1,3,2048]{2,1,0:T(4,128)} %get-tuple-element.49) | copy-start | bytes 73732
  279.6 14.8 %copy-start.31 = (f32[1,3,2048]{2,1,0:T(4,128)S(1)}, f32[1,3,2048]{2,1,0:T(4,128)}, u32[]{:S(2)}) copy-start(f32[1,3,2048]{2,1,0:T(4,128)} %get-tuple-element.50) | copy-start | bytes 73732
  279.6 15.4 %copy-start.30 = (f32[1,3,2048]{2,1,0:T(4,128)S(1)}, f32[1,3,2048]{2,1,0:T(4,128)}, u32[]{:S(2)}) copy-start(f32[1,3,2048]{2,1,0:T(4,128)} %get-tuple-element.51) | copy-start | bytes 73732
  279.6 16.0 %copy-start.29 = (f32[1,3,2048]{2,1,0:T(4,128)S(1)}, f32[1,3,2048]{2,1,0:T(4,128)}, u32[]{:S(2)}) copy-start(f32[1,3,2048]{2,1,0:T(4,128)} %get-tuple-element.52) | copy-start | bytes 73732
  279.6 16.7 %copy-start.28 = (f32[1,3,2048]{2,1,0:T(4,128)S(1)}, f32[1,3,2048]{2,1,0:T(4,128)}, u32[]{:S(2)}) copy-start(f32[1,3,2048]{2,1,0:T(4,128)} %get-tuple-element.53) | copy-start | bytes 73732
  279.6 17.3 %copy-start.27 = (f32[1,3,2048]{2,1,0:T(4,128)S(1)}, f32[1,3,2048]{2,1,0:T(4,128)}, u32[]{:S(2)}) copy-start(f32[1,3,2048]{2,1,0:T(4,128)} %get-tuple-element.54) | copy-start | bytes 73732
  279.6 17.9 %copy-start.26 = (f32[1,3,2048]{2,1,0:T(4,128)S(1)}, f32[1,3,2048]{2,1,0:T(4,128)}, u32[]{:S(2)}) copy-start(f32[1,3,2048]{2,1,0:T(4,128)} %get-tuple-element.55) | copy-start | bytes 73732
  279.6 18.5 %copy-start.25 = (f32[1,3,2048]{2,1,0:T(4,128)S(1)}, f32[1,3,2048]{2,1,0:T(4,128)}, u32[]{:S(2)}) copy-start(f32[1,3,2048]{2,1,0:T(4,128)} %get-tuple-element.56) | copy-start | bytes 73732
  279.6 19.1 %copy-start.24 = (f32[1,3,2048]{2,1,0:T(4,128)S(1)}, f32[1,3,2048]{2,1,0:T(4,128)}, u32[]{:S(2)}) copy-start(f32[1,3,2048]{2,1,0:T(4,128)} %get-tuple-element.57) | copy-start | bytes 73732
  279.7 19.8 %copy-start.23 = (f32[1,3,2048]{2,1,0:T(4,128)S(1)}, f32[1,3,2048]{2,1,0:T(4,128)}, u32[]{:S(2)}) copy-start(f32[1,3,2048]{2,1,0:T(4,128)} %get-tuple-element.58) | copy-start | bytes 73732
  279.7 20.4 %copy-start.22 = (f32[1,3,2048]{2,1,0:T(4,128)S(1)}, f32[1,3,2048]{2,1,0:T(4,128)}, u32[]{:S(2)}) copy-start(f32[1,3,2048]{2,1,0:T(4,128)} %get-tuple-element.59) | copy-start | bytes 73732
  281.1 19.6 %copy-start.21 = (f32[1,3,2048]{2,1,0:T(4,128)S(1)}, f32[1,3,2048]{2,1,0:T(4,128)}, u32[]{:S(2)}) copy-start(f32[1,3,2048]{2,1,0:T(4,128)} %get-tuple-element.60) | copy-start | bytes 73732
  281.1 20.2 %copy-start.20 = (f32[1,3,2048]{2,1,0:T(4,128)S(1)}, f32[1,3,2048]{2,1,0:T(4,128)}, u32[]{:S(2)}) copy-start(f32[1,3,2048]{2,1,0:T(4,128)} %get-tuple-element.61) | copy-start | bytes 73732
  281.1 20.9 %copy-start.19 = (f32[1,3,2048]{2,1,0:T(4,128)S(1)}, f32[1,3,2048]{2,1,0:T(4,128)}, u32[]{:S(2)}) copy-start(f32[1,3,2048]{2,1,0:T(4,128)} %get-tuple-element.62) | copy-start | bytes 73732
  281.1 21.5 %copy-start.18 = (f32[1,3,2048]{2,1,0:T(4,128)S(1)}, f32[1,3,2048]{2,1,0:T(4,128)}, u32[]{:S(2)}) copy-start(f32[1,3,2048]{2,1,0:T(4,128)} %get-tuple-element.63) | copy-start | bytes 73732
  281.1 22.1 %copy-start.17 = (f32[1,3,2048]{2,1,0:T(4,128)S(1)}, f32[1,3,2048]{2,1,0:T(4,128)}, u32[]{:S(2)}) copy-start(f32[1,3,2048]{2,1,0:T(4,128)} %get-tuple-element.64) | copy-start | bytes 73732
  281.1 22.7 %copy-start.16 = (f32[1,3,2048]{2,1,0:T(4,128)S(1)}, f32[1,3,2048]{2,1,0:T(4,128)}, u32[]{:S(2)}) copy-start(f32[1,3,2048]{2,1,0:T(4,128)} %get-tuple-element.65) | copy-start | bytes 73732
  281.1 23.3 %copy-start.15 = (f32[1,3,2048]{2,1,0:T(4,128)S(1)}, f32[1,3,2048]{2,1,0:T(4,128)}, u32[]{:S(2)}) copy-start(f32[1,3,2048]{2,1,0:T(4,128)} %get-tuple-element.66) | copy-start | bytes 73732
  281.1 24.0 %copy-start.14 = (f32[1,3,2048]{2,1,0:T(4,128)S(1)}, f32[1,3,2048]{2,1,0:T(4,128)}, u32[]{:S(2)}) copy-start(f32[1,3,2048]{2,1,0:T(4,128)} %get-tuple-element.67) | copy-start | bytes 73732
  281.1 24.6 %copy-start.13 = (f32[1,3,2048]{2,1,0:T(4,128)S(1)}, f32[1,3,2048]{2,1,0:T(4,128)}, u32[]{:S(2)}) copy-start(f32[1,3,2048]{2,1,0:T(4,128)} %get-tuple-element.68) | copy-start | bytes 73732
  281.1 25.2 %copy-start.12 = (f32[1,3,2048]{2,1,0:T(4,128)S(1)}, f32[1,3,2048]{2,1,0:T(4,128)}, u32[]{:S(2)}) copy-start(f32[1,3,2048]{2,1,0:T(4,128)} %get-tuple-element.69) | copy-start | bytes 73732
  281.1 25.8 %copy-start.11 = (f32[1,3,2048]{2,1,0:T(4,128)S(1)}, f32[1,3,2048]{2,1,0:T(4,128)}, u32[]{:S(2)}) copy-start(f32[1,3,2048]{2,1,0:T(4,128)} %get-tuple-element.70) | copy-start | bytes 73732
  281.1 26.4 %copy-start.10 = (f32[1,3,2048]{2,1,0:T(4,128)S(1)}, f32[1,3,2048]{2,1,0:T(4,128)}, u32[]{:S(2)}) copy-start(f32[1,3,2048]{2,1,0:T(4,128)} %get-tuple-element.71) | copy-start | bytes 73732
  281.2 27.0 %copy-start.9 = (f32[1,3,2048]{2,1,0:T(4,128)S(1)}, f32[1,3,2048]{2,1,0:T(4,128)}, u32[]{:S(2)}) copy-start(f32[1,3,2048]{2,1,0:T(4,128)} %get-tuple-element.72) | copy-start | bytes 73732
  281.2 27.7 %copy-start.8 = (f32[1,3,2048]{2,1,0:T(4,128)S(1)}, f32[1,3,2048]{2,1,0:T(4,128)}, u32[]{:S(2)}) copy-start(f32[1,3,2048]{2,1,0:T(4,128)} %get-tuple-element.73) | copy-start | bytes 73732
  281.2 28.3 %copy-start.7 = (f32[1,3,2048]{2,1,0:T(4,128)S(1)}, f32[1,3,2048]{2,1,0:T(4,128)}, u32[]{:S(2)}) copy-start(f32[1,3,2048]{2,1,0:T(4,128)} %get-tuple-element.74) | copy-start | bytes 73732
  281.2 28.9 %copy-start.6 = (f32[1,3,2048]{2,1,0:T(4,128)S(1)}, f32[1,3,2048]{2,1,0:T(4,128)}, u32[]{:S(2)}) copy-start(f32[1,3,2048]{2,1,0:T(4,128)} %get-tuple-element.75) | copy-start | bytes 73732
  284.9 35.2 %collective-permute-start.3 = (f32[3,10,1,512]{3,2,1,0:T(1,128)}, f32[3,10,1,512]{3,2,1,0:T(1,128)S(1)}, u32[]{:S(2)}, u32[]{:S(2)}) collective-permute-start(f32[3,10,1,512]{3,2,1,0:T(1,128)} %get-tuple-element.231), channel_id=1, source_target_pairs={{0,1},{1,2},{2,3},{3,4},{4,5},{5,6},{6,7},{8,9},{9,10},{10,11},{11... | collective-permute-start | bytes 184328 | tf_op jit(solution)/shard_map/ppermute | solution.py:28
  288.4 31.7 %collective-permute-start.2 = (f32[3,10,1,512]{3,2,1,0:T(1,128)}, f32[3,10,1,512]{3,2,1,0:T(1,128)S(1)}, u32[]{:S(2)}, u32[]{:S(2)}) collective-permute-start(f32[3,10,1,512]{3,2,1,0:T(1,128)} %get-tuple-element.232), channel_id=1, source_target_pairs={{1,0},{2,1},{3,2},{4,3},{5,4},{6,5},{7,6},{9,8},{10,9},{11,10},{12... | collective-permute-start | bytes 184328 | tf_op jit(solution)/shard_map/ppermute | solution.py:29
  320.1 4.2 copy-start.1
  320.1 4.2 copy-start.2
  320.1 4.2 copy-start.3
  320.2 4.2 copy-start.4
  328.0 7.5 collective-permute-start.5
  331.1 7.4 collective-permute-start.4
  338.7 7.2 collective-permute-start.7
  343.7 5.5 collective-permute-start.6
  353.5 6.6 collective-permute-start.9
  356.3 8.0 collective-permute-start.8
  364.4 6.8 collective-permute-start.11
  368.8 5.5 collective-permute-start.10
where the time goes:
time: 961 us; the launch traced here: 942 us
  other arithmetic  524 us (55%)
  local copies, waits for them, and re-layouts  332 us (35%)
  starting transfers between devices  62.7 us (7%)
  waiting for transfers between devices  20.1 us (2%)
    scatter-add x1, other arithmetic, per_device(): step_rows = stepped.reshape(3, -1).T.at[cell_index].add(arrived_rows)  491 us
    gather x2, local copies, waits for them, and re-layouts, per_device(): taken = jnp.transpose(cell_rows[wanted], (0, 2, 1))  149 us
    unnamed x92, local copies, waits for them, and re-layouts  75 us
    add x1, local copies, waits for them, and re-layouts, outer_step(): third_part * velocity  32.6 us
    ppermute x6, starting transfers between devices, extended(): before = lax.ppermute(last, axis, up)  22.1 us
    sub x32, local copies, waits for them, and re-layouts, thomas(): following = reduced_d[level] - reduced_c[level][None] * following  20 us
  transfers between devices with their start and end apart: 15, of which 7 were waited for; matrix products, arithmetic and copies ran while one was open for 28% of the time, Pallas kernels for 0%

commit v1 on v0

v1 whole, which is shorter than its diff:
```python
import jax
import jax.numpy as jnp
import numpy as np
from jax import lax
from jax.experimental import pallas as pl
from jax.experimental.pallas import tpu as pltpu
from jax.sharding import PartitionSpec as P

MESH = pl.DeviceIdType.MESH
BF16, F32, I32 = jnp.bfloat16, jnp.float32, jnp.int32

DEVICES = 128
SLOTS = 32
TILE = 128
TILES = 16
LEVELS = 32
CX, CY, ZB = 8, 32, 4
XY = CX * CY
NZ = 512
TOP = 8
MIB = 1 << 20

time_step = 0.1
viscosity = 0.001
smag_coef = 0.02
kappa_coef = 0.41
damping_plus = 26.0
stretch = 1.12
area_ratio = 4.0

FRAC = (stretch ** np.arange(LEVELS + 2) - 1.0) / (stretch ** (LEVELS + 1) - 1.0)
SPACING = FRAC[1:] - FRAC[:-1]
FACE = 0.5 * (FRAC[1:] + FRAC[:-1])
SPAN = 0.5 * (FRAC[2:] - FRAC[:-2])
LOWER = [float(v) for v in time_step / (SPACING[:-1] * SPAN)]
UPPER = [float(v) for v in time_step / (SPACING[1:] * SPAN)]


def dot_nn(a, b):
    return lax.dot_general(a, b, (((1,), (0,)), ((), ())), preferred_element_type=F32)


def dot_nt(a, b):
    return lax.dot_general(a, b, (((1,), (1,)), ((), ())), preferred_element_type=F32)


def split(value):
    high = value.astype(BF16)
    return high, (value - high.astype(F32)).astype(BF16)


def columns(j):
    return pl.ds(j * TILE, TILE)


def build_request(owner, cell, onehot, rank, picked, message):
    rows = lax.broadcasted_iota(I32, (TILE, TILE), 0)
    lanes = lax.broadcasted_iota(I32, (TILE, TILE), 1)
    earlier = jnp.where(rows < lanes, 1.0, 0.0).astype(BF16)
    summing = jnp.concatenate([earlier, jnp.ones((TILE, TILE), BF16)], axis=1)
    slots = lax.broadcasted_iota(I32, (SLOTS, TILE), 0)
    taken = jnp.zeros((TILE, TILE), F32)
    for j in range(TILES):
        mine = rows == owner[j : j + 1, :]
        one = jnp.where(mine, 1.0, 0.0).astype(BF16)
        onehot[:, columns(j)] = one
        counts = dot_nn(one, summing)
        place = jnp.sum(jnp.where(mine, counts[:, :TILE] + taken, 0.0), axis=0, keepdims=True).astype(I32)
        taken = taken + counts[:, TILE:]
        rank[j : j + 1, :] = place
        at = cell[j : j + 1, :]
        slot = slots == place
        depth = at & (NZ - 1)
        for part, value in enumerate((at >> 9, depth & (NZ - 2), depth & 1)):
            picked[part * SLOTS : (part + 1) * SLOTS, columns(j)] = jnp.where(slot, value.astype(F32), 0.0).astype(BF16)
    message[:, 0, :] = dot_nt(onehot[...], picked[...])


def read_request(arrived, request):
    turned = arrived[:, 0, :].T
    request[0:SLOTS, :] = turned[0:SLOTS].astype(I32)
    request[SLOTS : 2 * SLOTS, :] = (turned[SLOTS : 2 * SLOTS] + turned[2 * SLOTS : 3 * SLOTS]).astype(I32)


def gather_cells(request, depth_hot, v_high, v_low, gathered, message):
    depths = lax.broadcasted_iota(I32, (NZ, TILE), 0)
    planes = lax.broadcasted_iota(I32, (XY, TILE), 0)

    @pl.loop(0, SLOTS // 2)
    def _(pair):
        for half in range(2):
            slot = pair * 2 + half
            row = request[pl.ds(SLOTS + slot, 1), :]
            depth_hot[pair, :, columns(half)] = jnp.where(depths == row, 1.0, 0.0).astype(BF16)
        hot = depth_hot[pair]
        for c in range(3):
            part = pl.ds(c * XY, XY)
            found = dot_nn(v_high[part, :], hot) + dot_nn(v_low[part, :], hot)
            for half in range(2):
                slot = pair * 2 + half
                where = planes == request[pl.ds(slot, 1), :]
                gathered[pl.ds(c * SLOTS + slot, 1), :] = jnp.sum(
                    jnp.where(where, found[:, half * TILE : (half + 1) * TILE], 0.0), axis=0, keepdims=True
                )

    message[:, 0, :] = gathered[...].T


def scatter_cells(request, depth_hot, arrived, pushes, a_high, a_low, base, out):
    planes = lax.broadcasted_iota(I32, (XY, TILE), 0)
    pushes[...] = arrived[:, 0, :].T

    @pl.loop(0, 3)
    def _(c):
        for slot in range(SLOTS):
            where = planes == request[slot : slot + 1, :]
            push = pushes[pl.ds(c * SLOTS + slot, 1), :]
            high = push.astype(BF16).astype(F32)
            low = push - high
            a_high[slot // 2, :, columns(slot % 2)] = jnp.where(where, high, 0.0).astype(BF16)
            a_low[slot // 2, :, columns(slot % 2)] = jnp.where(where, low, 0.0).astype(BF16)
        for side in range(2):
            total = jnp.zeros((XY, 256), F32)
            for pair in range(SLOTS // 2):
                hot = depth_hot[pair, side * 256 : (side + 1) * 256, :]
                total = total + dot_nt(a_high[pair], hot) + dot_nt(a_low[pair], hot)
            for half in range(2):
                zb = side * 2 + half
                for x in range(CX):
                    block = total[x * CY : (x + 1) * CY, half * TILE : (half + 1) * TILE]
                    out[c, x, zb] = base[c, x, zb] + block


def prepare(field, v_high, v_low):
    @pl.loop(0, 3 * CX)
    def _(i):
        c, x = i // CX, i % CX
        for zb in range(ZB):
            high, low = split(field[c, x + 1, zb, TOP : TOP + CY, :])
            rows = pl.ds(pl.multiple_of(i * CY, CY), CY)
            v_high[rows, columns(zb)] = high
            v_low[rows, columns(zb)] = low


def pack_rows(field, edge):
    for side, row in ((0, TOP), (1, TOP + CY - 1)):
        for c in range(3):
            for x in range(CX):
                edge[side, c * CX + x] = field[c, x + 1, :, row, :]


def unpack_rows(field, edge, span, spans, slab, slabs):
    for side, row in ((0, TOP - 1), (1, TOP + CY)):
        for c in range(3):
            for x in range(CX):
                field[c, x + 1, :, row, :] = edge[side, c * CX + x]
    zero_row = jnp.zeros((CX, ZB, TILE), F32)
    zero_plane = jnp.zeros((ZB, CY, TILE), F32)
    for c in range(3):

        @pl.when(span == 0)
        def _():
            field[c, 1 : CX + 1, :, TOP - 1, :] = zero_row

        @pl.when(span == spans - 1)
        def _():
            field[c, 1 : CX + 1, :, TOP + CY, :] = zero_row

        @pl.when(slab == 0)
        def _():
            field[c, 0, :, TOP : TOP + CY, :] = zero_plane

        @pl.when(slab == slabs - 1)
        def _():
            field[c, CX + 1, :, TOP : TOP + CY, :] = zero_plane


def stage(field, first, out, out_x, out_top, keep, mix):
    lane = lax.broadcasted_iota(I32, (8, TILE), 1)
    at_start, at_end = lane == 0, lane == TILE - 1
    zeros = jnp.zeros((8, TILE), F32)

    @pl.loop(0, CX)
    def _(x):
        for y in range(0, CY, 8):
            here = pl.ds(TOP + y, 8)
            center = [[field[c, x + 1, zb, here, :] for zb in range(ZB)] for c in range(3)]
            ahead = [[pltpu.roll(v, TILE - 1, 1) for v in row] for row in center]
            behind = [[pltpu.roll(v, 1, 1) for v in row] for row in center]
            for zb in range(ZB):
                mid = [center[c][zb] for c in range(3)]
                shear = zeros
                lap, grads = [], []
                for c in range(3):
                    xp, xm = field[c, x + 2, zb, here, :], field[c, x, zb, here, :]
                    yp, ym = field[c, x + 1, zb, pl.ds(TOP + y + 1, 8), :], field[c, x + 1, zb, pl.ds(TOP + y - 1, 8), :]
                    zp = jnp.where(at_end, ahead[c][zb + 1] if zb + 1 < ZB else zeros, ahead[c][zb])
                    zm = jnp.where(at_start, behind[c][zb - 1] if zb else zeros, behind[c][zb])
                    gx, gy, gz = xp - xm, yp - ym, zp - zm
                    shear = shear + (gx * gx + gy * gy + gz * gz)
                    lap.append(((xp + xm) + (yp + ym)) + ((zp + zm) - 6.0 * mid[c]))
                    grads.append(mid[0] * gx + mid[1] * gy + mid[2] * gz)
                eddy = viscosity + (0.5 * smag_coef) * jnp.sqrt(shear)
                for c in range(3):
                    moved = mid[c] + time_step * (eddy * lap[c] - 0.5 * grads[c])
                    if keep:
                        moved = keep * first[c, x + 1, zb, here, :] + mix * moved
                    out[c, x + out_x, zb, pl.ds(out_top + y, 8), :] = moved


def tangential(vector, normal):
    along = vector[0] * normal[0] + vector[1] * normal[1] + vector[2] * normal[2]
    return [vector[c] - along * normal[c] for c in range(3)]


def level(ref, c, k):
    return ref[c, pl.ds(k, TILES, stride=LEVELS), :]


def diffusivity(first, height, inverse2):
    ratio = float((viscosity / FRAC[1]) ** 2)
    square = (first[0] * first[0] + first[1] * first[1] + first[2] * first[2]) * inverse2 * ratio
    scaled = height * jnp.sqrt(jnp.sqrt(square))

    def at(k):
        damping = 1.0 - jnp.exp(scaled * float(-FACE[k] / (viscosity * damping_plus)))
        return viscosity + (float(kappa_coef * FACE[k]) * scaled) * (damping * damping)

    return at


def sweep_one(profile, height, inverse2, forcing, kept):
    at = diffusivity([level(profile, c, 0) for c in range(3)], height, inverse2)
    above = at(LEVELS)
    ratio = jnp.zeros((TILES, TILE), F32)
    value = [jnp.zeros((TILES, TILE), F32)] * 3
    answer = jnp.ones((TILES, TILE), F32)
    for k in range(LEVELS - 1, -1, -1):
        below = at(k)
        low = (below * inverse2) * LOWER[k]
        up = (above * inverse2) * UPPER[k]
        inverse = 1.0 / (1.0 + low + up * (1.0 - ratio))
        ratio = low * inverse
        value = [(level(profile, c, k) - time_step * forcing[c] + up * value[c]) * inverse for c in range(3)]
        answer = answer * (up * inverse)
        above = below
    for c in range(3):
        kept[c] = value[c]
    kept[3] = answer


def sweep_two(profile, height, inverse2, forcing, target, kept, ratios, values):
    at = diffusivity([kept[c] + kept[3] * target[c] for c in range(3)], height, inverse2)
    above = at(LEVELS)
    ratio = jnp.zeros((TILES, TILE), F32)
    value = target
    for k in range(LEVELS - 1, -1, -1):
        below = at(k)
        low = (below * inverse2) * LOWER[k]
        up = (above * inverse2) * UPPER[k]
        inverse = 1.0 / (1.0 + low + up * (1.0 - ratio))
        ratio = low * inverse
        ratios[k] = ratio
        value = [(level(profile, c, k) - time_step * forcing[c] + up * value[c]) * inverse for c in range(3)]
        for c in range(3):
            values[c, k] = value[c]
        above = below
    return value


def substitute(ratios, values, result):
    value = [values[c, 0] for c in range(3)]
    for k in range(LEVELS):
        if k:
            value = [values[c, k] + ratios[k] * value[c] for c in range(3)]
        for c in range(3):
            result[c, pl.ds(k, TILES, stride=LEVELS), :] = value[c]


def take_matched(arrived, onehot, rank, matched):
    high, low = split(arrived[:, 0, :].T)
    slots = lax.broadcasted_iota(I32, (SLOTS, TILE), 0)
    for j in range(TILES):
        one = onehot[:, columns(j)]
        found = dot_nn(high, one) + dot_nn(low, one)
        slot = slots == rank[j : j + 1, :]
        for c in range(3):
            matched[c, j : j + 1, :] = jnp.sum(
                jnp.where(slot, found[c * SLOTS : (c + 1) * SLOTS], 0.0), axis=0, keepdims=True
            )


def send_stress(stress, onehot, rank, picked, picked_low, message):
    slots = lax.broadcasted_iota(I32, (SLOTS, TILE), 0)
    for j in range(TILES):
        slot = slots == rank[j : j + 1, :]
        for c in range(3):
            push = (-time_step * area_ratio) * stress[c, j : j + 1, :]
            high = push.astype(BF16).astype(F32)
            rows = slice(c * SLOTS, (c + 1) * SLOTS)
            picked[rows, columns(j)] = jnp.where(slot, high, 0.0).astype(BF16)
            picked_low[rows, columns(j)] = jnp.where(slot, push - high, 0.0).astype(BF16)
    message[:, 0, :] = dot_nt(onehot[...], picked[...]) + dot_nt(onehot[...], picked_low[...])


def kernel(
    velocity, profile_in, normal_in, height_in, pressure_in, owner, cell,
    new_velocity, wall_profile, wall_stress,
    field_0, field_1, field_2, stepped, v_high, v_low, depth_hot, a_high, a_low,
    onehot, rank, picked, picked_low, request, gathered,
    profile, result, ratios, values, vectors, kept,
    outgoing, incoming, edge_out, edge_in,
    load_sem, profile_sem, store_sem, row_send, row_recv, halo_send, halo_recv,
):
    slab, span = lax.axis_index("slab"), lax.axis_index("span")
    slabs, spans = 16, 8
    me = slab * spans + span
    fields = (field_0, field_1, field_2)

    loads = [
        pltpu.make_async_copy(
            velocity.at[:, :, :, columns(zb)], field_0.at[:, pl.ds(1, CX), zb, pl.ds(TOP, CY), :], load_sem.at[zb]
        )
        for zb in range(ZB)
    ]
    for copy in loads:
        copy.start()
    profile_loads = [
        pltpu.make_async_copy(
            profile_in.at[:, :, columns(j)], profile.at[:, pl.ds(j * LEVELS, LEVELS), :], profile_sem.at[j]
        )
        for j in range(TILES)
    ]
    for copy in profile_loads:
        copy.start()

    barrier = pltpu.get_barrier_semaphore()

    @pl.loop(1, DEVICES)
    def _(i):
        other = lax.rem(me + i, DEVICES)
        pl.semaphore_signal(barrier, 1, device_id=(other // spans, lax.rem(other, spans)), device_id_type=MESH)

    def send_rows(phase):
        @pl.loop(1, DEVICES)
        def _(i):
            other = lax.rem(me + i, DEVICES)
            pltpu.make_async_remote_copy(
                src_ref=outgoing.at[phase, other],
                dst_ref=incoming.at[phase, me],
                send_sem=row_send.at[phase],
                recv_sem=row_recv.at[phase],
                device_id=(other // spans, lax.rem(other, spans)),
                device_id_type=MESH,
            ).start()

        incoming[phase, me] = outgoing[phase, me]

    def await_rows(phase):
        rows = outgoing.at[phase, pl.ds(0, DEVICES - 1)]
        pltpu.make_async_copy(rows, rows, row_send.at[phase]).wait()
        rows = incoming.at[phase, pl.ds(0, DEVICES - 1)]
        pltpu.make_async_copy(rows, rows, row_recv.at[phase]).wait()

    up_x = (lax.rem(slab + 1, slabs), span)
    down_x = (lax.rem(slab + slabs - 1, slabs), span)
    up_y = (slab, lax.rem(span + 1, spans))
    down_y = (slab, lax.rem(span + spans - 1, spans))

    def halo(n):
        field = fields[n]
        inner = pl.ds(TOP, CY)
        ends = (
            (field.at[:, CX, :, inner, :], field.at[:, 0, :, inner, :], up_x),
            (field.at[:, 1, :, inner, :], field.at[:, CX + 1, :, inner, :], down_x),
            (edge_out.at[n, 1], edge_in.at[n, 0], up_y),
            (edge_out.at[n, 0], edge_in.at[n, 1], down_y),
        )
        return [
            pltpu.make_async_remote_copy(
                src_ref=src, dst_ref=dst, send_sem=halo_send.at[n, i], recv_sem=halo_recv.at[n, i],
                device_id=to, device_id_type=MESH,
            )
            for i, (src, dst, to) in enumerate(ends)
        ]

    def send_halo(n):
        pack_rows(fields[n], edge_out.at[n])
        copies = halo(n)
        for copy in copies:
            copy.start()
        return copies

    def await_halo(n, copies):
        for copy in copies:
            copy.wait()
        unpack_rows(fields[n], edge_in.at[n], span, spans, slab, slabs)

    build_request(owner, cell, onehot, rank, picked, outgoing.at[0])
    for copy in loads:
        copy.wait()
    pl.semaphore_wait(barrier, DEVICES - 1)
    send_rows(0)
    copies = send_halo(0)

    for copy in profile_loads:
        copy.wait()
    normal, pressure, matched = vectors.at[0], vectors.at[1], vectors.at[2]
    for c in range(3):
        for j in range(TILES):
            normal[c, j : j + 1, :] = normal_in[c : c + 1, columns(j)]
            pressure[c, j : j + 1, :] = pressure_in[c : c + 1, columns(j)]
    height = height_in[...]
    inverse2 = 1.0 / (height * height)
    forcing = tangential([pressure[c] for c in range(3)], [normal[c] for c in range(3)])
    sweep_one(profile, height, inverse2, forcing, kept)
    prepare(field_0, v_high, v_low)
    await_halo(0, copies)
    stage(field_0, field_0, field_1, 1, TOP, None, None)
    copies = send_halo(1)

    await_rows(0)
    read_request(incoming.at[0], request)
    gather_cells(request, depth_hot, v_high, v_low, gathered, outgoing.at[1])
    send_rows(1)

    await_halo(1, copies)
    stage(field_1, field_0, field_2, 1, TOP, 0.75, 0.25)
    copies = send_halo(2)

    await_rows(1)
    take_matched(incoming.at[1], onehot, rank, matched)
    target = tangential([matched[c] for c in range(3)], [normal[c] for c in range(3)])
    forcing = tangential([pressure[c] for c in range(3)], [normal[c] for c in range(3)])
    first = sweep_two(profile, height, inverse2, forcing, target, kept, ratios, values)
    scale = float(viscosity / FRAC[1]) / height
    stress = vectors.at[3]
    for c in range(3):
        stress[c] = first[c] * scale
    send_stress(stress, onehot, rank, picked, picked_low, outgoing.at[2])
    send_rows(2)

    for c in range(3):
        for j in range(TILES):
            wall_stress[c : c + 1, columns(j)] = stress[c, j : j + 1, :]
    substitute(ratios, values, result)
    profile_stores = [
        pltpu.make_async_copy(
            result.at[:, pl.ds(j * LEVELS, LEVELS), :], wall_profile.at[:, :, columns(j)], profile_sem.at[j]
        )
        for j in range(TILES)
    ]
    for copy in profile_stores:
        copy.start()
    await_halo(2, copies)
    stage(field_2, field_0, stepped, 0, 0, 1.0 / 3.0, 2.0 / 3.0)

    await_rows(2)
    scatter_cells(request, depth_hot, incoming.at[2], gathered, a_high, a_low, stepped, stepped)
    stores = [
        pltpu.make_async_copy(stepped.at[:, :, zb], new_velocity.at[:, :, :, columns(zb)], store_sem.at[zb])
        for zb in range(ZB)
    ]
    for copy in stores:
        copy.start()
    for copy in profile_stores + stores:
        copy.wait()


def per_device(velocity, profile, normal, height, pressure_grad, owner_device, match_cell):
    padded = pltpu.VMEM((3, CX + 2, ZB, CY + 16, TILE), F32)
    hbm, vmem = pl.BlockSpec(memory_space=pl.ANY), pl.BlockSpec(memory_space=pltpu.VMEM)
    new_velocity, wall_profile, wall_stress = pl.pallas_call(
        kernel,
        out_shape=(
            jax.ShapeDtypeStruct(velocity.shape, F32),
            jax.ShapeDtypeStruct((3, LEVELS, TILES * TILE), F32),
            jax.ShapeDtypeStruct((3, TILES * TILE), F32),
        ),
        in_specs=[hbm, hbm, vmem, vmem, vmem, vmem, vmem],
        out_specs=(hbm, hbm, vmem),
        scratch_shapes=[
            padded, padded, padded,
            pltpu.VMEM((3, CX, ZB, CY, TILE), F32),
            pltpu.VMEM((3 * XY, NZ), BF16), pltpu.VMEM((3 * XY, NZ), BF16),
            pltpu.VMEM((SLOTS // 2, NZ, 2 * TILE), BF16),
            pltpu.VMEM((SLOTS // 2, XY, 2 * TILE), BF16), pltpu.VMEM((SLOTS // 2, XY, 2 * TILE), BF16),
            pltpu.VMEM((DEVICES, TILES * TILE), BF16),
            pltpu.VMEM((TILES, TILE), I32),
            pltpu.VMEM((DEVICES, TILES * TILE), BF16), pltpu.VMEM((DEVICES, TILES * TILE), BF16),
            pltpu.VMEM((2 * SLOTS, TILE), I32),
            pltpu.VMEM((DEVICES, TILE), F32),
            pltpu.VMEM((3, TILES * LEVELS, TILE), F32), pltpu.VMEM((3, TILES * LEVELS, TILE), F32),
            pltpu.VMEM((LEVELS, TILES, TILE), F32), pltpu.VMEM((3, LEVELS, TILES, TILE), F32),
            pltpu.VMEM((4, 3, TILES, TILE), F32), pltpu.VMEM((4, TILES, TILE), F32),
            pltpu.VMEM((3, DEVICES, 1, TILE), F32), pltpu.VMEM((3, DEVICES, 1, TILE), F32),
            pltpu.VMEM((3, 2, 3 * CX, ZB, TILE), F32), pltpu.VMEM((3, 2, 3 * CX, ZB, TILE), F32),
            pltpu.SemaphoreType.DMA((ZB,)), pltpu.SemaphoreType.DMA((TILES,)), pltpu.SemaphoreType.DMA((ZB,)),
            pltpu.SemaphoreType.DMA((3,)), pltpu.SemaphoreType.DMA((3,)),
            pltpu.SemaphoreType.DMA((3, 4)), pltpu.SemaphoreType.DMA((3, 4)),
        ],
        compiler_params=pltpu.CompilerParams(
            collective_id=0, has_side_effects=True, vmem_limit_bytes=52 * MIB
        ),
    )(
        velocity,
        jnp.transpose(profile, (1, 0, 2)),
        normal,
        height.reshape(TILES, TILE),
        pressure_grad,
        owner_device.reshape(TILES, TILE),
        match_cell.reshape(TILES, TILE),
    )
    return new_velocity, jnp.transpose(wall_profile, (1, 0, 2)), wall_stress


def solution(mesh):
    return jax.shard_map(
        per_device,
        mesh=mesh,
        in_specs=(
            P(None, "slab", "span", None),
            P(None, None, ("slab", "span")),
            P(None, ("slab", "span")),
            P(("slab", "span")),
            P(None, ("slab", "span")),
            P(("slab", "span"), None),
            P(("slab", "span")),
        ),
        out_specs=(
            P(None, "slab", "span", None),
            P(None, None, ("slab", "span")),
            P(None, ("slab", "span")),
        ),
        check_vma=False,
    )
```

time: 961 us -> 67.9 us (0.07)
  the two profiles are of different devices: /device:TPU:13 before, /device:TPU:1 now
where the time goes in v1:
time: 67.9 us; the launch traced here: 67.5 us
  Pallas kernels  57.9 us (85%)
  local copies, waits for them, and re-layouts  8.97 us (13%)
    pallas_call x1, Pallas kernels, per_device(): pl.pallas_call(kernel, out_shape=(jax.ShapeDtypeStruct(velocity.shape, F3...  57.9 us
    unnamed x15, local copies, waits for them, and re-layouts  8.97 us

profile of v1, /device:TPU:1, one launch (start us, length us, event | category | flops | bytes accessed | tf_op | source)
XLA Modules:
  0.0 67.5 jit_solution(14130236001758680447)
XLA Ops:
  0.6 0.0 copy-start
  0.6 1.1 %copy-done = f32[32,3,2048]{2,0,1:T(8,128)S(1)} copy-done((f32[32,3,2048]{2,0,1:T(8,128)S(1)}, f32[32,3,2048]{2,0,1:T(8,128)}, u32[]{:S(2)}) %copy-start) | copy-done | bytes 786456
  1.8 0.0 copy-start.1
  1.8 0.8 %copy-done.1 = f32[3,2048]{1,0:T(4,128)S(1)} copy-done((f32[3,2048]{1,0:T(4,128)S(1)}, f32[3,2048]{1,0:T(4,128)}, u32[]{:S(2)}) %copy-start.1) | copy-done | bytes 24600
  2.5 0.0 copy-start.2
  2.5 0.8 %copy-done.2 = f32[3,2048]{1,0:T(4,128)S(1)} copy-done((f32[3,2048]{1,0:T(4,128)S(1)}, f32[3,2048]{1,0:T(4,128)}, u32[]{:S(2)}) %copy-start.2) | copy-done | bytes 24600
  3.3 0.0 copy-start.3
  3.3 0.7 %copy-done.3 = f32[2048]{0:T(1024)S(1)} copy-done((f32[2048]{0:T(1024)S(1)}, f32[2048]{0:T(1024)}, u32[]{:S(2)}) %copy-start.3) | copy-done | bytes 8216
  4.0 0.0 copy-start.4
  4.0 0.7 %copy-done.4 = s32[2048,1]{0,1:T(1,128)S(1)} copy-done((s32[2048,1]{0,1:T(1,128)S(1)}, s32[2048,1]{0,1:T(1,128)}, u32[]{:S(2)}) %copy-start.4) | copy-done | bytes 8216
  4.7 0.0 copy-start.5
  4.7 0.7 %copy-done.5 = s32[2048]{0:T(1024)S(1)} copy-done((s32[2048]{0:T(1024)S(1)}, s32[2048]{0:T(1024)}, u32[]{:S(2)}) %copy-start.5) | copy-done | bytes 8216
  5.4 57.9 %shard_map.94 = (f32[3,8,32,512]{3,2,1,0:T(8,128)}, f32[3,32,2048]{2,1,0:T(8,128)S(1)}, f32[3,2048]{1,0:T(4,128)S(1)}) custom-call(f32[3,8,32,512]{3,2,1,0:T(8,128)} %velocity.1, f32[3,32,2048]{2,1,0:T(8,128)S(1)} %bitcast.6, f32[3,2048]{1,0:T(4,128)S(1)} %copy-done.1, f32[16,128]{1,0:T(8,128)S(1)} %bitcast.7, f32[3,2048]{1,0:T(4,128)S(1)} %copy-done.2, ...), custom_call_target="tpu_custom_call" | custom-call | tf_op jit(solution)/shard_map/pallas_call | solution.py:473
  63.2 2.7 %copy.13 = f32[3,8,32,512]{3,2,1,0:T(8,128)} copy(f32[3,8,32,512]{3,2,1,0:T(8,128)} %get-tuple-element.12) | data formatting | bytes 3145728
  66.0 0.9 %copy.14 = f32[32,3,2048]{2,0,1:T(8,128)} copy(f32[32,3,2048]{2,0,1:T(8,128)S(1)} %bitcast.5) | data formatting | bytes 1572864
  66.9 0.6 copy.15
Async XLA Ops:
  0.6 1.1 %copy-start = (f32[32,3,2048]{2,0,1:T(8,128)S(1)}, f32[32,3,2048]{2,0,1:T(8,128)}, u32[]{:S(2)}) copy-start(f32[32,3,2048]{2,0,1:T(8,128)} %param.8) | copy-start | bytes 2359300
  1.8 0.8 %copy-start.1 = (f32[3,2048]{1,0:T(4,128)S(1)}, f32[3,2048]{1,0:T(4,128)}, u32[]{:S(2)}) copy-start(f32[3,2048]{1,0:T(4,128)} %normal_in.1) | copy-start | bytes 73732
  2.5 0.8 %copy-start.2 = (f32[3,2048]{1,0:T(4,128)S(1)}, f32[3,2048]{1,0:T(4,128)}, u32[]{:S(2)}) copy-start(f32[3,2048]{1,0:T(4,128)} %pressure_in.1) | copy-start | bytes 73732
  3.3 0.7 %copy-start.3 = (f32[2048]{0:T(1024)S(1)}, f32[2048]{0:T(1024)}, u32[]{:S(2)}) copy-start(f32[2048]{0:T(1024)} %param.10) | copy-start | bytes 24580
  4.0 0.7 %copy-start.4 = (s32[2048,1]{0,1:T(1,128)S(1)}, s32[2048,1]{0,1:T(1,128)}, u32[]{:S(2)}) copy-start(s32[2048,1]{0,1:T(1,128)} %param.12) | copy-start | bytes 24580
  4.7 0.7 %copy-start.5 = (s32[2048]{0:T(1024)S(1)}, s32[2048]{0:T(1024)}, u32[]{:S(2)}) copy-start(s32[2048]{0:T(1024)} %param.13) | copy-start | bytes 24580

commit v2 on v1

--- a/solution.py
+++ b/solution.py
@@ -19,6 +19,7 @@
 NZ = 512
 TOP = 8
 MIB = 1 << 20
+EARLY = 5
 
 time_step = 0.1
 viscosity = 0.001
@@ -59,6 +60,7 @@
     earlier = jnp.where(rows < lanes, 1.0, 0.0).astype(BF16)
     summing = jnp.concatenate([earlier, jnp.ones((TILE, TILE), BF16)], axis=1)
     slots = lax.broadcasted_iota(I32, (SLOTS, TILE), 0)
+    picked[3 * SLOTS :, :] = jnp.zeros((SLOTS, TILES * TILE), BF16)
     taken = jnp.zeros((TILE, TILE), F32)
     for j in range(TILES):
         mine = rows == owner[j : j + 1, :]
@@ -82,17 +84,18 @@
     request[SLOTS : 2 * SLOTS, :] = (turned[SLOTS : 2 * SLOTS] + turned[2 * SLOTS : 3 * SLOTS]).astype(I32)
 
 
-def gather_cells(request, depth_hot, v_high, v_low, gathered, message):
+def gather_cells(request, v_high, v_low, gathered, begin, end):
     depths = lax.broadcasted_iota(I32, (NZ, TILE), 0)
     planes = lax.broadcasted_iota(I32, (XY, TILE), 0)
 
-    @pl.loop(0, SLOTS // 2)
+    @pl.loop(begin, end)
     def _(pair):
+        hots = []
         for half in range(2):
             slot = pair * 2 + half
             row = request[pl.ds(SLOTS + slot, 1), :]
-            depth_hot[pair, :, columns(half)] = jnp.where(depths == row, 1.0, 0.0).astype(BF16)
-        hot = depth_hot[pair]
+            hots.append(jnp.where(depths == row, 1.0, 0.0).astype(BF16))
+        hot = jnp.concatenate(hots, axis=1)
         for c in range(3):
             part = pl.ds(c * XY, XY)
             found = dot_nn(v_high[part, :], hot) + dot_nn(v_low[part, :], hot)
@@ -103,32 +106,36 @@
                     jnp.where(where, found[:, half * TILE : (half + 1) * TILE], 0.0), axis=0, keepdims=True
                 )
 
-    message[:, 0, :] = gathered[...].T
-
-
-def scatter_cells(request, depth_hot, arrived, pushes, a_high, a_low, base, out):
-    planes = lax.broadcasted_iota(I32, (XY, TILE), 0)
-    pushes[...] = arrived[:, 0, :].T
-
-    @pl.loop(0, 3)
-    def _(c):
+
+def scatter_kernel(requests, stresses, base, wall_in, stress_in, out, wall_out, stress_out, depth_hot, pushes, planes_of):
+    c = pl.program_id(0)
+    wall_out[...] = wall_in[...]
+
+    @pl.when(c == 0)
+    def _():
+        stress_out[...] = stress_in[...]
+        pushes[...] = stresses[...].T
+        planes_of[...] = requests[...].T[0:SLOTS]
+        depths = lax.broadcasted_iota(I32, (TILE, NZ), 1)
+        depth = (requests[:, SLOTS : 2 * SLOTS] + requests[:, 2 * SLOTS : 3 * SLOTS]).astype(I32)
         for slot in range(SLOTS):
-            where = planes == request[slot : slot + 1, :]
-            push = pushes[pl.ds(c * SLOTS + slot, 1), :]
-            high = push.astype(BF16).astype(F32)
-            low = push - high
-            a_high[slot // 2, :, columns(slot % 2)] = jnp.where(where, high, 0.0).astype(BF16)
-            a_low[slot // 2, :, columns(slot % 2)] = jnp.where(where, low, 0.0).astype(BF16)
-        for side in range(2):
-            total = jnp.zeros((XY, 256), F32)
-            for pair in range(SLOTS // 2):
-                hot = depth_hot[pair, side * 256 : (side + 1) * 256, :]
-                total = total + dot_nt(a_high[pair], hot) + dot_nt(a_low[pair], hot)
-            for half in range(2):
-                zb = side * 2 + half
-                for x in range(CX):
-                    block = total[x * CY : (x + 1) * CY, half * TILE : (half + 1) * TILE]
-                    out[c, x, zb] = base[c, x, zb] + block
+            hot = jnp.where(depths == depth[:, slot : slot + 1], 1.0, 0.0).astype(BF16)
+            depth_hot[slot // 2, columns(slot % 2), :] = hot
+
+    planes = lax.broadcasted_iota(I32, (XY, TILE), 0).astype(F32).astype(BF16)
+    zero = jnp.zeros((), BF16)
+    total = jnp.zeros((XY, NZ), F32)
+    for pair in range(SLOTS // 2):
+        highs, lows = [], []
+        for slot in (2 * pair, 2 * pair + 1):
+            high, low = split(pushes[pl.ds(c * SLOTS + slot, 1), :])
+            where = planes == planes_of[slot : slot + 1, :].astype(BF16)
+            highs.append(jnp.where(where, high, zero))
+            lows.append(jnp.where(where, low, zero))
+        for part in (highs, lows):
+            total = total + dot_nn(jnp.concatenate(part, axis=1), depth_hot[pair])
+    for x in range(CX):
+        out[0, x] = base[0, x] + total[x * CY : (x + 1) * CY]
 
 
 def prepare(field, v_high, v_low):
@@ -149,39 +156,38 @@
                 edge[side, c * CX + x] = field[c, x + 1, :, row, :]
 
 
-def unpack_rows(field, edge, span, spans, slab, slabs):
+def unpack_rows(field, edge, span, spans):
     for side, row in ((0, TOP - 1), (1, TOP + CY)):
         for c in range(3):
             for x in range(CX):
                 field[c, x + 1, :, row, :] = edge[side, c * CX + x]
     zero_row = jnp.zeros((CX, ZB, TILE), F32)
+    for at, row in ((0, TOP - 1), (spans - 1, TOP + CY)):
+
+        @pl.when(span == at)
+        def _():
+            for c in range(3):
+                field[c, 1 : CX + 1, :, row, :] = zero_row
+
+
+def clear_planes(field, slab, slabs):
     zero_plane = jnp.zeros((ZB, CY, TILE), F32)
-    for c in range(3):
-
-        @pl.when(span == 0)
+    for at, plane in ((0, 0), (slabs - 1, CX + 1)):
+
+        @pl.when(slab == at)
         def _():
-            field[c, 1 : CX + 1, :, TOP - 1, :] = zero_row
-
-        @pl.when(span == spans - 1)
-        def _():
-            field[c, 1 : CX + 1, :, TOP + CY, :] = zero_row
-
-        @pl.when(slab == 0)
-        def _():
-            field[c, 0, :, TOP : TOP + CY, :] = zero_plane
-
-        @pl.when(slab == slabs - 1)
-        def _():
-            field[c, CX + 1, :, TOP : TOP + CY, :] = zero_plane
-
-
-def stage(field, first, out, out_x, out_top, keep, mix):
+            for c in range(3):
+                field[c, plane, :, TOP : TOP + CY, :] = zero_plane
+
+
+def stage(field, first, store, keep, mix, planes):
     lane = lax.broadcasted_iota(I32, (8, TILE), 1)
     at_start, at_end = lane == 0, lane == TILE - 1
     zeros = jnp.zeros((8, TILE), F32)
 
-    @pl.loop(0, CX)
-    def _(x):
+    @pl.loop(0, len(planes))
+    def _(i):
+        x = planes.start + i * planes.step
         for y in range(0, CY, 8):
             here = pl.ds(TOP + y, 8)
             center = [[field[c, x + 1, zb, here, :] for zb in range(ZB)] for c in range(3)]
@@ -205,7 +211,7 @@
                     moved = mid[c] + time_step * (eddy * lap[c] - 0.5 * grads[c])
                     if keep:
                         moved = keep * first[c, x + 1, zb, here, :] + mix * moved
-                    out[c, x + out_x, zb, pl.ds(out_top + y, 8), :] = moved
+                    store(c, x, y, zb, moved)
 
 
 def tangential(vector, normal):
@@ -291,6 +297,7 @@
 
 
 def send_stress(stress, onehot, rank, picked, picked_low, message):
+    picked_low[3 * SLOTS :, :] = jnp.zeros((SLOTS, TILES * TILE), BF16)
     slots = lax.broadcasted_iota(I32, (SLOTS, TILE), 0)
     for j in range(TILES):
         slot = slots == rank[j : j + 1, :]
@@ -304,18 +311,39 @@
 
 
 def kernel(
-    velocity, profile_in, normal_in, height_in, pressure_in, owner, cell,
-    new_velocity, wall_profile, wall_stress,
-    field_0, field_1, field_2, stepped, v_high, v_low, depth_hot, a_high, a_low,
+    velocity, profile_in, normal_in, height_in, pressure_in, owner_in, cell_in,
+    stepped_out, wall_profile, wall_stress, requests, stresses,
+    field_0, field_1, field_2, stepped, v_high, v_low,
     onehot, rank, picked, picked_low, request, gathered,
     profile, result, ratios, values, vectors, kept,
+    owner, cell, height_v, normal_v, pressure_v,
     outgoing, incoming, edge_out, edge_in,
-    load_sem, profile_sem, store_sem, row_send, row_recv, halo_send, halo_recv,
+    small_sem, load_sem, profile_sem, store_sem, row_send, row_recv, halo_send, halo_recv,
 ):
     slab, span = lax.axis_index("slab"), lax.axis_index("span")
     slabs, spans = 16, 8
     me = slab * spans + span
     fields = (field_0, field_1, field_2)
+    barrier = pltpu.get_barrier_semaphore()
+
+    small = [
+        pltpu.make_async_copy(src, dst, small_sem.at[i])
+        for i, (src, dst) in enumerate(
+            ((owner_in, owner), (cell_in, cell), (height_in, height_v), (normal_in, normal_v), (pressure_in, pressure_v))
+        )
+    ]
+    for copy in small:
+        copy.start()
+
+    @pl.loop(0, slabs)
+    def _(i):
+        to = lax.rem(slab + i, slabs)
+        for j in range(1, spans):
+            pl.semaphore_signal(barrier, 1, device_id=(to, lax.rem(span + j, spans)), device_id_type=MESH)
+
+    @pl.loop(1, slabs)
+    def _(i):
+        pl.semaphore_signal(barrier, 1, device_id=(lax.rem(slab + i, slabs), span), device_id_type=MESH)
 
     loads = [
         pltpu.make_async_copy(
@@ -334,32 +362,36 @@
     for copy in profile_loads:
         copy.start()
 
-    barrier = pltpu.get_barrier_semaphore()
-
-    @pl.loop(1, DEVICES)
-    def _(i):
-        other = lax.rem(me + i, DEVICES)
-        pl.semaphore_signal(barrier, 1, device_id=(other // spans, lax.rem(other, spans)), device_id_type=MESH)
+    arrivals = (incoming.at[0], incoming.at[1], stresses)
+
+    def send_row(phase, to_slab, to_span):
+        pltpu.make_async_remote_copy(
+            src_ref=outgoing.at[phase, to_slab * spans + to_span],
+            dst_ref=arrivals[phase].at[me],
+            send_sem=row_send.at[phase],
+            recv_sem=row_recv.at[phase],
+            device_id=(to_slab, to_span),
+            device_id_type=MESH,
+        ).start()
 
     def send_rows(phase):
-        @pl.loop(1, DEVICES)
-        def _(i):
-            other = lax.rem(me + i, DEVICES)
-            pltpu.make_async_remote_copy(
-                src_ref=outgoing.at[phase, other],
-                dst_ref=incoming.at[phase, me],
-                send_sem=row_send.at[phase],
-                recv_sem=row_recv.at[phase],
-                device_id=(other // spans, lax.rem(other, spans)),
-                device_id_type=MESH,
-            ).start()
-
-        incoming[phase, me] = outgoing[phase, me]
+        for across in (2, 1, 3, 0):
+
+            @pl.loop(1 if across == 0 else 0, 4)
+            def _(i):
+                to = lax.rem(slab + across * 4 + i, slabs)
+                for j in range(spans):
+                    send_row(phase, to, lax.rem(span + j, spans))
+
+        for j in range(1, spans):
+            send_row(phase, slab, lax.rem(span + j, spans))
+        if phase < 2:
+            incoming[phase, me] = outgoing[phase, me]
 
     def await_rows(phase):
         rows = outgoing.at[phase, pl.ds(0, DEVICES - 1)]
         pltpu.make_async_copy(rows, rows, row_send.at[phase]).wait()
-        rows = incoming.at[phase, pl.ds(0, DEVICES - 1)]
+        rows = arrivals[phase].at[pl.ds(0, DEVICES - 1)]
         pltpu.make_async_copy(rows, rows, row_recv.at[phase]).wait()
 
     up_x = (lax.rem(slab + 1, slabs), span)
@@ -367,7 +399,7 @@
     up_y = (slab, lax.rem(span + 1, spans))
     down_y = (slab, lax.rem(span + spans - 1, spans))
 
-    def halo(n):
+    def send_halo(n):
         field = fields[n]
         inner = pl.ds(TOP, CY)
         ends = (
@@ -376,26 +408,41 @@
             (edge_out.at[n, 1], edge_in.at[n, 0], up_y),
             (edge_out.at[n, 0], edge_in.at[n, 1], down_y),
         )
-        return [
+        copies = [
             pltpu.make_async_remote_copy(
                 src_ref=src, dst_ref=dst, send_sem=halo_send.at[n, i], recv_sem=halo_recv.at[n, i],
                 device_id=to, device_id_type=MESH,
             )
             for i, (src, dst, to) in enumerate(ends)
         ]
-
-    def send_halo(n):
-        pack_rows(fields[n], edge_out.at[n])
-        copies = halo(n)
-        for copy in copies:
+        for copy in copies[:2]:
+            copy.start()
+        pack_rows(field, edge_out.at[n])
+        for copy in copies[2:]:
             copy.start()
         return copies
 
-    def await_halo(n, copies):
-        for copy in copies:
+    def await_y(n, copies):
+        for copy in copies[2:]:
             copy.wait()
-        unpack_rows(fields[n], edge_in.at[n], span, spans, slab, slabs)
-
+        unpack_rows(fields[n], edge_in.at[n], span, spans)
+
+    def await_x(n, copies):
+        for copy in copies[:2]:
+            copy.wait()
+        clear_planes(fields[n], slab, slabs)
+
+    def into(field):
+        def store(c, x, y, zb, value):
+            field[c, x + 1, zb, pl.ds(TOP + y, 8), :] = value
+
+        return store
+
+    def into_result(c, x, y, zb, value):
+        stepped[c, x, zb, pl.ds(y, 8), :] = value
+
+    for copy in small[:2]:
+        copy.wait()
     build_request(owner, cell, onehot, rank, picked, outgoing.at[0])
     for copy in loads:
         copy.wait()
@@ -403,29 +450,36 @@
     send_rows(0)
     copies = send_halo(0)
 
-    for copy in profile_loads:
+    for copy in small[2:] + profile_loads:
         copy.wait()
     normal, pressure, matched = vectors.at[0], vectors.at[1], vectors.at[2]
     for c in range(3):
         for j in range(TILES):
-            normal[c, j : j + 1, :] = normal_in[c : c + 1, columns(j)]
-            pressure[c, j : j + 1, :] = pressure_in[c : c + 1, columns(j)]
-    height = height_in[...]
+            normal[c, j : j + 1, :] = normal_v[c : c + 1, columns(j)]
+            pressure[c, j : j + 1, :] = pressure_v[c : c + 1, columns(j)]
+    height = height_v[...]
     inverse2 = 1.0 / (height * height)
     forcing = tangential([pressure[c] for c in range(3)], [normal[c] for c in range(3)])
     sweep_one(profile, height, inverse2, forcing, kept)
     prepare(field_0, v_high, v_low)
-    await_halo(0, copies)
-    stage(field_0, field_0, field_1, 1, TOP, None, None)
-    copies = send_halo(1)
+    await_y(0, copies)
+    stage(field_0, field_0, into(field_1), None, None, range(1, CX - 1))
 
     await_rows(0)
     read_request(incoming.at[0], request)
-    gather_cells(request, depth_hot, v_high, v_low, gathered, outgoing.at[1])
+    keep_requests = pltpu.make_async_copy(incoming.at[0], requests, store_sem.at[0])
+    keep_requests.start()
+    gather_cells(request, v_high, v_low, gathered, 0, EARLY)
+    await_x(0, copies)
+    stage(field_0, field_0, into(field_1), None, None, range(0, CX, CX - 1))
+    copies = send_halo(1)
+    gather_cells(request, v_high, v_low, gathered, EARLY, SLOTS // 2)
+    outgoing[1, :, 0, :] = gathered[...].T
     send_rows(1)
 
-    await_halo(1, copies)
-    stage(field_1, field_0, field_2, 1, TOP, 0.75, 0.25)
+    await_y(1, copies)
+    await_x(1, copies)
+    stage(field_1, field_0, into(field_2), 0.75, 0.25, range(0, CX))
     copies = send_halo(2)
 
     await_rows(1)
@@ -439,10 +493,21 @@
         stress[c] = first[c] * scale
     send_stress(stress, onehot, rank, picked, picked_low, outgoing.at[2])
     send_rows(2)
+    own_row = pltpu.make_async_copy(outgoing.at[2, me], stresses.at[me], store_sem.at[1])
+    own_row.start()
 
     for c in range(3):
         for j in range(TILES):
             wall_stress[c : c + 1, columns(j)] = stress[c, j : j + 1, :]
+    await_y(2, copies)
+    await_x(2, copies)
+    stage(field_2, field_0, into_result, 1.0 / 3.0, 2.0 / 3.0, range(0, CX))
+    stores = [
+        pltpu.make_async_copy(stepped.at[:, :, zb], stepped_out.at[:, :, :, columns(zb)], load_sem.at[zb])
+        for zb in range(ZB)
+    ]
+    for copy in stores:
+        copy.start()
     substitute(ratios, values, result)
     profile_stores = [
         pltpu.make_async_copy(
@@ -452,39 +517,26 @@
     ]
     for copy in profile_stores:
         copy.start()
-    await_halo(2, copies)
-    stage(field_2, field_0, stepped, 0, 0, 1.0 / 3.0, 2.0 / 3.0)
-
+    for copy in [keep_requests, own_row] + stores + profile_stores:
+        copy.wait()
     await_rows(2)
-    scatter_cells(request, depth_hot, incoming.at[2], gathered, a_high, a_low, stepped, stepped)
-    stores = [
-        pltpu.make_async_copy(stepped.at[:, :, zb], new_velocity.at[:, :, :, columns(zb)], store_sem.at[zb])
-        for zb in range(ZB)
-    ]
-    for copy in stores:
-        copy.start()
-    for copy in profile_stores + stores:
-        copy.wait()
 
 
 def per_device(velocity, profile, normal, height, pressure_grad, owner_device, match_cell):
     padded = pltpu.VMEM((3, CX + 2, ZB, CY + 16, TILE), F32)
-    hbm, vmem = pl.BlockSpec(memory_space=pl.ANY), pl.BlockSpec(memory_space=pltpu.VMEM)
-    new_velocity, wall_profile, wall_stress = pl.pallas_call(
+    hbm, vmem = pl.BlockSpec(memory_space=pltpu.HBM), pl.BlockSpec(memory_space=pltpu.VMEM)
+    wall_shape = jax.ShapeDtypeStruct((3, LEVELS, TILES * TILE), F32)
+    stress_shape = jax.ShapeDtypeStruct((3, TILES * TILE), F32)
+    rows_shape = jax.ShapeDtypeStruct((DEVICES, 1, TILE), F32)
+    stepped, wall_profile, wall_stress, requests, stresses = pl.pallas_call(
         kernel,
-        out_shape=(
-            jax.ShapeDtypeStruct(velocity.shape, F32),
-            jax.ShapeDtypeStruct((3, LEVELS, TILES * TILE), F32),
-            jax.ShapeDtypeStruct((3, TILES * TILE), F32),
-        ),
-        in_specs=[hbm, hbm, vmem, vmem, vmem, vmem, vmem],
-        out_specs=(hbm, hbm, vmem),
+        out_shape=(jax.ShapeDtypeStruct(velocity.shape, F32), wall_shape, stress_shape, rows_shape, rows_shape),
+        in_specs=[hbm] * 7,
+        out_specs=(hbm, hbm, vmem, hbm, hbm),
         scratch_shapes=[
             padded, padded, padded,
             pltpu.VMEM((3, CX, ZB, CY, TILE), F32),
             pltpu.VMEM((3 * XY, NZ), BF16), pltpu.VMEM((3 * XY, NZ), BF16),
-            pltpu.VMEM((SLOTS // 2, NZ, 2 * TILE), BF16),
-            pltpu.VMEM((SLOTS // 2, XY, 2 * TILE), BF16), pltpu.VMEM((SLOTS // 2, XY, 2 * TILE), BF16),
             pltpu.VMEM((DEVICES, TILES * TILE), BF16),
             pltpu.VMEM((TILES, TILE), I32),
             pltpu.VMEM((DEVICES, TILES * TILE), BF16), pltpu.VMEM((DEVICES, TILES * TILE), BF16),
@@ -493,14 +545,16 @@
             pltpu.VMEM((3, TILES * LEVELS, TILE), F32), pltpu.VMEM((3, TILES * LEVELS, TILE), F32),
             pltpu.VMEM((LEVELS, TILES, TILE), F32), pltpu.VMEM((3, LEVELS, TILES, TILE), F32),
             pltpu.VMEM((4, 3, TILES, TILE), F32), pltpu.VMEM((4, TILES, TILE), F32),
+            pltpu.VMEM((TILES, TILE), I32), pltpu.VMEM((TILES, TILE), I32), pltpu.VMEM((TILES, TILE), F32),
+            pltpu.VMEM((3, TILES * TILE), F32), pltpu.VMEM((3, TILES * TILE), F32),
             pltpu.VMEM((3, DEVICES, 1, TILE), F32), pltpu.VMEM((3, DEVICES, 1, TILE), F32),
             pltpu.VMEM((3, 2, 3 * CX, ZB, TILE), F32), pltpu.VMEM((3, 2, 3 * CX, ZB, TILE), F32),
-            pltpu.SemaphoreType.DMA((ZB,)), pltpu.SemaphoreType.DMA((TILES,)), pltpu.SemaphoreType.DMA((ZB,)),
+            pltpu.SemaphoreType.DMA((5,)), pltpu.SemaphoreType.DMA((ZB,)), pltpu.SemaphoreType.DMA((TILES,)), pltpu.SemaphoreType.DMA((2,)),
             pltpu.SemaphoreType.DMA((3,)), pltpu.SemaphoreType.DMA((3,)),
             pltpu.SemaphoreType.DMA((3, 4)), pltpu.SemaphoreType.DMA((3, 4)),
         ],
         compiler_params=pltpu.CompilerParams(
-            collective_id=0, has_side_effects=True, vmem_limit_bytes=52 * MIB
+            collective_id=0, has_side_effects=True, vmem_limit_bytes=60 * MIB
         ),
     )(
         velocity,
@@ -511,6 +565,23 @@
         owner_device.reshape(TILES, TILE),
         match_cell.reshape(TILES, TILE),
     )
+    plane = pl.BlockSpec((1, CX, CY, NZ), lambda c: (c, 0, 0, 0))
+    walls = pl.BlockSpec((1, LEVELS, TILES * TILE), lambda c: (c, 0, 0))
+    whole = pl.BlockSpec((DEVICES, TILE), lambda c: (0, 0))
+    whole_stress = pl.BlockSpec((3, TILES * TILE), lambda c: (0, 0))
+    new_velocity, wall_profile, wall_stress = pl.pallas_call(
+        scatter_kernel,
+        grid=(3,),
+        out_shape=(jax.ShapeDtypeStruct(velocity.shape, F32), wall_shape, stress_shape),
+        in_specs=[whole, whole, plane, walls, whole_stress],
+        out_specs=(plane, walls, whole_stress),
+        scratch_shapes=[
+            pltpu.VMEM((SLOTS // 2, 2 * TILE, NZ), BF16),
+            pltpu.VMEM((DEVICES, TILE), F32),
+            pltpu.VMEM((SLOTS, TILE), F32),
+        ],
+        compiler_params=pltpu.CompilerParams(vmem_limit_bytes=60 * MIB),
+    )(requests.reshape(DEVICES, TILE), stresses.reshape(DEVICES, TILE), stepped, wall_profile, wall_stress)
     return new_velocity, jnp.transpose(wall_profile, (1, 0, 2)), wall_stress
 
 

time: 67.9 us -> 52.5 us (0.77)
  local copies, waits for them, and re-layouts: 8.97 us -> 0 us
  Pallas kernels: 57.9 us -> 51.7 us
    pallas_call x1, Pallas kernels: 57.9 us -> 41.8 us  [per_device(): pl.pallas_call(kernel, out_shape=(jax.ShapeDtypeStruct(velocity.shape, F3...]
    pallas_call x0 -> x1, Pallas kernels: none -> 9.91 us  [per_device(): pl.pallas_call(scatter_kernel, grid=(3,), out_shape=(jax.ShapeDtypeStruct...]
    unnamed x15 -> x0, local copies, waits for them, and re-layouts: 8.97 us -> none
where the time goes in v2:
time: 52.5 us; the launch traced here: 52.4 us
  Pallas kernels  51.7 us (98%)
  between operations  0.64 us (1%)
    pallas_call x1, Pallas kernels, per_device(): pl.pallas_call(kernel, out_shape=(jax.ShapeDtypeStruct(velocity.shape, F3...  41.8 us
    pallas_call x1, Pallas kernels, per_device(): pl.pallas_call(scatter_kernel, grid=(3,), out_shape=(jax.ShapeDtypeStruct...  9.91 us

profile of v2, /device:TPU:1, one launch (start us, length us, event | category | flops | bytes accessed | tf_op | source)
XLA Modules:
  0.0 52.4 jit_solution(6563220346618936446)
XLA Ops:
  0.6 41.8 %shard_map.94 = (f32[3,8,32,512]{3,2,1,0:T(8,128)}, f32[3,32,2048]{2,1,0:T(8,128)}, f32[3,2048]{1,0:T(4,128)}, f32[128,1,128]{2,1,0:T(1,128)}, f32[128,1,128]{2,1,0:T(1,128)}) custom-call(f32[3,8,32,512]{3,2,1,0:T(8,128)} %velocity.1, f32[3,32,2048]{2,1,0:T(8,128)} %bitcast.7, f32[3,2048]{1,0:T(4,128)} %normal_in.1, f32[16,128]{1,0:T(8,128)} %bitcast.10, ...), custom_call_target="tpu_custom_call" | custom-call | tf_op jit(solution)/shard_map/pallas_call | solution.py:531
  42.5 9.9 %shard_map.95 = (f32[3,8,32,512]{3,2,1,0:T(8,128)}, f32[3,32,2048]{2,1,0:T(8,128)}, f32[3,2048]{1,0:T(4,128)}) custom-call(f32[128,128]{1,0:T(8,128)} %bitcast.8, f32[128,128]{1,0:T(8,128)} %bitcast.9, f32[3,8,32,512]{3,2,1,0:T(8,128)} %get-tuple-element.13.base, f32[3,32,2048]{2,1,0:T(8,128)} %get-tuple-element.14.wall_in, ...), custom_call_target="tpu_custom_call" | custom-call | tf_op jit(solution)/shard_map/pallas_call | solution.py:572

commit v3 on v2

--- a/solution.py
+++ b/solution.py
@@ -19,7 +19,8 @@
 NZ = 512
 TOP = 8
 MIB = 1 << 20
-EARLY = 5
+INNER, OUTER = range(1, CX - 1), range(0, CX, CX - 1)
+EARLY = 6
 
 time_step = 0.1
 viscosity = 0.001
@@ -84,27 +85,27 @@
     request[SLOTS : 2 * SLOTS, :] = (turned[SLOTS : 2 * SLOTS] + turned[2 * SLOTS : 3 * SLOTS]).astype(I32)
 
 
-def gather_cells(request, v_high, v_low, gathered, begin, end):
+def gather_cells(request, v_high, v_low, gathered, begin, end, step):
     depths = lax.broadcasted_iota(I32, (NZ, TILE), 0)
     planes = lax.broadcasted_iota(I32, (XY, TILE), 0)
 
-    @pl.loop(begin, end)
-    def _(pair):
-        hots = []
-        for half in range(2):
-            slot = pair * 2 + half
-            row = request[pl.ds(SLOTS + slot, 1), :]
-            hots.append(jnp.where(depths == row, 1.0, 0.0).astype(BF16))
-        hot = jnp.concatenate(hots, axis=1)
-        for c in range(3):
-            part = pl.ds(c * XY, XY)
-            found = dot_nn(v_high[part, :], hot) + dot_nn(v_low[part, :], hot)
-            for half in range(2):
-                slot = pair * 2 + half
-                where = planes == request[pl.ds(slot, 1), :]
-                gathered[pl.ds(c * SLOTS + slot, 1), :] = jnp.sum(
-                    jnp.where(where, found[:, half * TILE : (half + 1) * TILE], 0.0), axis=0, keepdims=True
-                )
+    @pl.loop(begin, end, step=step)
+    def _(first):
+        for i in range(step):
+            pair = first + i
+            slots = (2 * pair, 2 * pair + 1)
+            hots = [
+                jnp.where(depths == request[pl.ds(SLOTS + slot, 1), :], 1.0, 0.0).astype(BF16) for slot in slots
+            ]
+            hot = jnp.concatenate(hots, axis=1)
+            for c in range(3):
+                part = slice(c * XY, (c + 1) * XY)
+                found = dot_nn(v_high[part, :], hot) + dot_nn(v_low[part, :], hot)
+                for half, slot in enumerate(slots):
+                    where = planes == request[pl.ds(slot, 1), :]
+                    gathered[pl.ds(c * SLOTS + slot, 1), :] = jnp.sum(
+                        jnp.where(where, found[:, half * TILE : (half + 1) * TILE], 0.0), axis=0, keepdims=True
+                    )
 
 
 def scatter_kernel(requests, stresses, base, wall_in, stress_in, out, wall_out, stress_out, depth_hot, pushes, planes_of):
@@ -235,6 +236,11 @@
     return at
 
 
+def reciprocal(value):
+    guess = pl.reciprocal(value, approx=True)
+    return guess * (2.0 - value * guess)
+
+
 def sweep_one(profile, height, inverse2, forcing, kept):
     at = diffusivity([level(profile, c, 0) for c in range(3)], height, inverse2)
     above = at(LEVELS)
@@ -245,7 +251,7 @@
         below = at(k)
         low = (below * inverse2) * LOWER[k]
         up = (above * inverse2) * UPPER[k]
-        inverse = 1.0 / (1.0 + low + up * (1.0 - ratio))
+        inverse = reciprocal(1.0 + low + up * (1.0 - ratio))
         ratio = low * inverse
         value = [(level(profile, c, k) - time_step * forcing[c] + up * value[c]) * inverse for c in range(3)]
         answer = answer * (up * inverse)
@@ -264,7 +270,7 @@
         below = at(k)
         low = (below * inverse2) * LOWER[k]
         up = (above * inverse2) * UPPER[k]
-        inverse = 1.0 / (1.0 + low + up * (1.0 - ratio))
+        inverse = reciprocal(1.0 + low + up * (1.0 - ratio))
         ratio = low * inverse
         ratios[k] = ratio
         value = [(level(profile, c, k) - time_step * forcing[c] + up * value[c]) * inverse for c in range(3)]
@@ -318,7 +324,7 @@
     profile, result, ratios, values, vectors, kept,
     owner, cell, height_v, normal_v, pressure_v,
     outgoing, incoming, edge_out, edge_in,
-    small_sem, load_sem, profile_sem, store_sem, row_send, row_recv, halo_send, halo_recv,
+    small_sem, load_sem, profile_sem, store_sem, plane_sem, row_send, row_recv, halo_send, halo_recv,
 ):
     slab, span = lax.axis_index("slab"), lax.axis_index("span")
     slabs, spans = 16, 8
@@ -399,7 +405,7 @@
     up_y = (slab, lax.rem(span + 1, spans))
     down_y = (slab, lax.rem(span + spans - 1, spans))
 
-    def send_halo(n):
+    def halo(n):
         field = fields[n]
         inner = pl.ds(TOP, CY)
         ends = (
@@ -408,19 +414,22 @@
             (edge_out.at[n, 1], edge_in.at[n, 0], up_y),
             (edge_out.at[n, 0], edge_in.at[n, 1], down_y),
         )
-        copies = [
+        return [
             pltpu.make_async_remote_copy(
                 src_ref=src, dst_ref=dst, send_sem=halo_send.at[n, i], recv_sem=halo_recv.at[n, i],
                 device_id=to, device_id_type=MESH,
             )
             for i, (src, dst, to) in enumerate(ends)
         ]
+
+    def send_x(copies):
         for copy in copies[:2]:
             copy.start()
-        pack_rows(field, edge_out.at[n])
+
+    def send_y(n, copies):
+        pack_rows(fields[n], edge_out.at[n])
         for copy in copies[2:]:
             copy.start()
-        return copies
 
     def await_y(n, copies):
         for copy in copies[2:]:
@@ -448,7 +457,9 @@
         copy.wait()
     pl.semaphore_wait(barrier, DEVICES - 1)
     send_rows(0)
-    copies = send_halo(0)
+    copies = halo(0)
+    send_y(0, copies)
+    send_x(copies)
 
     for copy in small[2:] + profile_loads:
         copy.wait()
@@ -463,24 +474,29 @@
     sweep_one(profile, height, inverse2, forcing, kept)
     prepare(field_0, v_high, v_low)
     await_y(0, copies)
-    stage(field_0, field_0, into(field_1), None, None, range(1, CX - 1))
+    stage(field_0, field_0, into(field_1), None, None, INNER)
 
     await_rows(0)
     read_request(incoming.at[0], request)
     keep_requests = pltpu.make_async_copy(incoming.at[0], requests, store_sem.at[0])
     keep_requests.start()
-    gather_cells(request, v_high, v_low, gathered, 0, EARLY)
+    gather_cells(request, v_high, v_low, gathered, 0, EARLY, 3)
     await_x(0, copies)
-    stage(field_0, field_0, into(field_1), None, None, range(0, CX, CX - 1))
-    copies = send_halo(1)
-    gather_cells(request, v_high, v_low, gathered, EARLY, SLOTS // 2)
+    stage(field_0, field_0, into(field_1), None, None, OUTER)
+    copies = halo(1)
+    send_x(copies)
+    send_y(1, copies)
+    gather_cells(request, v_high, v_low, gathered, EARLY, SLOTS // 2, 5)
     outgoing[1, :, 0, :] = gathered[...].T
     send_rows(1)
 
     await_y(1, copies)
+    stage(field_1, field_0, into(field_2), 0.75, 0.25, INNER)
     await_x(1, copies)
-    stage(field_1, field_0, into(field_2), 0.75, 0.25, range(0, CX))
-    copies = send_halo(2)
+    stage(field_1, field_0, into(field_2), 0.75, 0.25, OUTER)
+    copies = halo(2)
+    send_x(copies)
+    send_y(2, copies)
 
     await_rows(1)
     take_matched(incoming.at[1], onehot, rank, matched)
@@ -499,15 +515,22 @@
     for c in range(3):
         for j in range(TILES):
             wall_stress[c : c + 1, columns(j)] = stress[c, j : j + 1, :]
+    def store_planes(number, begin, count):
+        copies = [
+            pltpu.make_async_copy(
+                stepped.at[:, pl.ds(begin, count), zb],
+                stepped_out.at[:, pl.ds(begin, count), :, columns(zb)],
+                plane_sem.at[number, zb],
+            )
+            for zb in range(ZB)
+        ]
+        for copy in copies:
+            copy.start()
+        return copies
+
     await_y(2, copies)
-    await_x(2, copies)
-    stage(field_2, field_0, into_result, 1.0 / 3.0, 2.0 / 3.0, range(0, CX))
-    stores = [
-        pltpu.make_async_copy(stepped.at[:, :, zb], stepped_out.at[:, :, :, columns(zb)], load_sem.at[zb])
-        for zb in range(ZB)
-    ]
-    for copy in stores:
-        copy.start()
+    stage(field_2, field_0, into_result, 1.0 / 3.0, 2.0 / 3.0, INNER)
+    stores = store_planes(0, 1, CX - 2)
     substitute(ratios, values, result)
     profile_stores = [
         pltpu.make_async_copy(
@@ -517,6 +540,9 @@
     ]
     for copy in profile_stores:
         copy.start()
+    await_x(2, copies)
+    stage(field_2, field_0, into_result, 1.0 / 3.0, 2.0 / 3.0, OUTER)
+    stores += store_planes(1, 0, 1) + store_planes(2, CX - 1, 1)
     for copy in [keep_requests, own_row] + stores + profile_stores:
         copy.wait()
     await_rows(2)
@@ -549,7 +575,7 @@
             pltpu.VMEM((3, TILES * TILE), F32), pltpu.VMEM((3, TILES * TILE), F32),
             pltpu.VMEM((3, DEVICES, 1, TILE), F32), pltpu.VMEM((3, DEVICES, 1, TILE), F32),
             pltpu.VMEM((3, 2, 3 * CX, ZB, TILE), F32), pltpu.VMEM((3, 2, 3 * CX, ZB, TILE), F32),
-            pltpu.SemaphoreType.DMA((5,)), pltpu.SemaphoreType.DMA((ZB,)), pltpu.SemaphoreType.DMA((TILES,)), pltpu.SemaphoreType.DMA((2,)),
+            pltpu.SemaphoreType.DMA((5,)), pltpu.SemaphoreType.DMA((ZB,)), pltpu.SemaphoreType.DMA((TILES,)), pltpu.SemaphoreType.DMA((2,)), pltpu.SemaphoreType.DMA((3, ZB)),
             pltpu.SemaphoreType.DMA((3,)), pltpu.SemaphoreType.DMA((3,)),
             pltpu.SemaphoreType.DMA((3, 4)), pltpu.SemaphoreType.DMA((3, 4)),
         ],

time: 52.5 us -> 50.7 us (0.966)
  Pallas kernels: 51.7 us -> 49.9 us
    pallas_call x1, Pallas kernels: 41.8 us -> 40 us  [per_device(): pl.pallas_call(kernel, out_shape=(jax.ShapeDtypeStruct(velocity.shape, F3...]
where the time goes in v3:
time: 50.7 us; the launch traced here: 50.6 us
  Pallas kernels  49.9 us (98%)
  between operations  0.64 us (1%)
    pallas_call x1, Pallas kernels, per_device(): pl.pallas_call(kernel, out_shape=(jax.ShapeDtypeStruct(velocity.shape, F3...  40 us
    pallas_call x1, Pallas kernels, per_device(): pl.pallas_call(scatter_kernel, grid=(3,), out_shape=(jax.ShapeDtypeStruct...  9.9 us

profile of v3, /device:TPU:1, one launch (start us, length us, event | category | flops | bytes accessed | tf_op | source)
XLA Modules:
  0.0 50.6 jit_solution(7764498540258822076)
XLA Ops:
  0.6 40.0 %shard_map.94 = (f32[3,8,32,512]{3,2,1,0:T(8,128)}, f32[3,32,2048]{2,1,0:T(8,128)}, f32[3,2048]{1,0:T(4,128)}, f32[128,1,128]{2,1,0:T(1,128)}, f32[128,1,128]{2,1,0:T(1,128)}) custom-call(f32[3,8,32,512]{3,2,1,0:T(8,128)} %velocity.1, f32[3,32,2048]{2,1,0:T(8,128)} %bitcast.7, f32[3,2048]{1,0:T(4,128)} %normal_in.1, f32[16,128]{1,0:T(8,128)} %bitcast.10, ...), custom_call_target="tpu_custom_call" | custom-call | tf_op jit(solution)/shard_map/pallas_call | solution.py:557
  40.6 9.9 %shard_map.95 = (f32[3,8,32,512]{3,2,1,0:T(8,128)}, f32[3,32,2048]{2,1,0:T(8,128)}, f32[3,2048]{1,0:T(4,128)}) custom-call(f32[128,128]{1,0:T(8,128)} %bitcast.8, f32[128,128]{1,0:T(8,128)} %bitcast.9, f32[3,8,32,512]{3,2,1,0:T(8,128)} %get-tuple-element.13.base, f32[3,32,2048]{2,1,0:T(8,128)} %get-tuple-element.14.wall_in, ...), custom_call_target="tpu_custom_call" | custom-call | tf_op jit(solution)/shard_map/pallas_call | solution.py:598

commit v4 on v3

--- a/solution.py
+++ b/solution.py
@@ -49,6 +49,14 @@
 def split(value):
     high = value.astype(BF16)
     return high, (value - high.astype(F32)).astype(BF16)
+
+
+def hops(offset):
+    slab, span = offset
+    return sum(min(step, 4 - step) for step in (slab // 4, slab % 4, span // 2)) + span % 2 / 2
+
+
+FARTHEST_FIRST = sorted(((i, j) for i in range(16) for j in range(8) if i or j), key=hops, reverse=True)
 
 
 def columns(j):
@@ -332,6 +340,13 @@
     fields = (field_0, field_1, field_2)
     barrier = pltpu.get_barrier_semaphore()
 
+    def others():
+        for i, j in FARTHEST_FIRST:
+            yield lax.rem(slab + i, slabs), lax.rem(span + j, spans)
+
+    for to in others():
+        pl.semaphore_signal(barrier, 1, device_id=to, device_id_type=MESH)
+
     small = [
         pltpu.make_async_copy(src, dst, small_sem.at[i])
         for i, (src, dst) in enumerate(
@@ -340,16 +355,6 @@
     ]
     for copy in small:
         copy.start()
-
-    @pl.loop(0, slabs)
-    def _(i):
-        to = lax.rem(slab + i, slabs)
-        for j in range(1, spans):
-            pl.semaphore_signal(barrier, 1, device_id=(to, lax.rem(span + j, spans)), device_id_type=MESH)
-
-    @pl.loop(1, slabs)
-    def _(i):
-        pl.semaphore_signal(barrier, 1, device_id=(lax.rem(slab + i, slabs), span), device_id_type=MESH)
 
     loads = [
         pltpu.make_async_copy(
@@ -381,16 +386,8 @@
         ).start()
 
     def send_rows(phase):
-        for across in (2, 1, 3, 0):
-
-            @pl.loop(1 if across == 0 else 0, 4)
-            def _(i):
-                to = lax.rem(slab + across * 4 + i, slabs)
-                for j in range(spans):
-                    send_row(phase, to, lax.rem(span + j, spans))
-
-        for j in range(1, spans):
-            send_row(phase, slab, lax.rem(span + j, spans))
+        for to in others():
+            send_row(phase, *to)
         if phase < 2:
             incoming[phase, me] = outgoing[phase, me]
 
@@ -568,7 +565,7 @@
             pltpu.VMEM((DEVICES, TILES * TILE), BF16), pltpu.VMEM((DEVICES, TILES * TILE), BF16),
             pltpu.VMEM((2 * SLOTS, TILE), I32),
             pltpu.VMEM((DEVICES, TILE), F32),
-            pltpu.VMEM((3, TILES * LEVELS, TILE), F32), pltpu.VMEM((3, TILES * LEVELS, TILE), F32),
+            pltpu.VMEM((3, (TILES + 1) * LEVELS, TILE), F32), pltpu.VMEM((3, (TILES + 1) * LEVELS, TILE), F32),
             pltpu.VMEM((LEVELS, TILES, TILE), F32), pltpu.VMEM((3, LEVELS, TILES, TILE), F32),
             pltpu.VMEM((4, 3, TILES, TILE), F32), pltpu.VMEM((4, TILES, TILE), F32),
             pltpu.VMEM((TILES, TILE), I32), pltpu.VMEM((TILES, TILE), I32), pltpu.VMEM((TILES, TILE), F32),

time: 50.7 us -> 49.5 us (0.976)
  Pallas kernels: 49.9 us -> 48.7 us
    pallas_call x1, Pallas kernels: 40 us -> 38.8 us  [per_device(): pl.pallas_call(kernel, out_shape=(jax.ShapeDtypeStruct(velocity.shape, F3...]
where the time goes in v4:
time: 49.5 us; the launch traced here: 49.3 us
  Pallas kernels  48.7 us (98%)
  between operations  0.64 us (1%)
    pallas_call x1, Pallas kernels, per_device(): pl.pallas_call(kernel, out_shape=(jax.ShapeDtypeStruct(velocity.shape, F3...  38.8 us
    pallas_call x1, Pallas kernels, per_device(): pl.pallas_call(scatter_kernel, grid=(3,), out_shape=(jax.ShapeDtypeStruct...  9.9 us

profile of v4, /device:TPU:1, one launch (start us, length us, event | category | flops | bytes accessed | tf_op | source)
XLA Modules:
  0.0 49.3 jit_solution(15431901979953415713)
XLA Ops:
  0.6 38.8 %shard_map.94 = (f32[3,8,32,512]{3,2,1,0:T(8,128)}, f32[3,32,2048]{2,1,0:T(8,128)}, f32[3,2048]{1,0:T(4,128)}, f32[128,1,128]{2,1,0:T(1,128)}, f32[128,1,128]{2,1,0:T(1,128)}) custom-call(f32[3,8,32,512]{3,2,1,0:T(8,128)} %velocity.1, f32[3,32,2048]{2,1,0:T(8,128)} %bitcast.7, f32[3,2048]{1,0:T(4,128)} %normal_in.1, f32[16,128]{1,0:T(8,128)} %bitcast.10, ...), custom_call_target="tpu_custom_call" | custom-call | tf_op jit(solution)/shard_map/pallas_call | solution.py:554
  39.4 9.9 %shard_map.95 = (f32[3,8,32,512]{3,2,1,0:T(8,128)}, f32[3,32,2048]{2,1,0:T(8,128)}, f32[3,2048]{1,0:T(4,128)}) custom-call(f32[128,128]{1,0:T(8,128)} %bitcast.8, f32[128,128]{1,0:T(8,128)} %bitcast.9, f32[3,8,32,512]{3,2,1,0:T(8,128)} %get-tuple-element.13.base, f32[3,32,2048]{2,1,0:T(8,128)} %get-tuple-element.14.wall_in, ...), custom_call_target="tpu_custom_call" | custom-call | tf_op jit(solution)/shard_map/pallas_call | solution.py:595

commit v5 on v4

--- a/solution.py
+++ b/solution.py
@@ -125,11 +125,15 @@
         stress_out[...] = stress_in[...]
         pushes[...] = stresses[...].T
         planes_of[...] = requests[...].T[0:SLOTS]
-        depths = lax.broadcasted_iota(I32, (TILE, NZ), 1)
-        depth = (requests[:, SLOTS : 2 * SLOTS] + requests[:, 2 * SLOTS : 3 * SLOTS]).astype(I32)
+        depths = lax.broadcasted_iota(I32, (TILE, 256), 1).astype(F32).astype(BF16)
+        depth = requests[:, SLOTS : 2 * SLOTS] + requests[:, 2 * SLOTS : 3 * SLOTS]
         for slot in range(SLOTS):
-            hot = jnp.where(depths == depth[:, slot : slot + 1], 1.0, 0.0).astype(BF16)
-            depth_hot[slot // 2, columns(slot % 2), :] = hot
+            for side in range(2):
+                here = depth[:, slot : slot + 1] - 256.0 * side
+                here = jnp.where((here >= 0.0) & (here < 256.0), here, -1.0)
+                here = jnp.broadcast_to(here, (TILE, 256)).astype(BF16)
+                hot = jnp.where(depths == here, jnp.ones((), BF16), jnp.zeros((), BF16))
+                depth_hot[slot // 2, columns(slot % 2), side * 256 : (side + 1) * 256] = hot
 
     planes = lax.broadcasted_iota(I32, (XY, TILE), 0).astype(F32).astype(BF16)
     zero = jnp.zeros((), BF16)

time: 49.5 us -> 49.4 us (level)
  no operation moved by 1% of the time
where the time goes in v5:
time: 49.4 us; the launch traced here: 49.3 us
  Pallas kernels  48.6 us (98%)
  between operations  0.64 us (1%)
    pallas_call x1, Pallas kernels, per_device(): pl.pallas_call(kernel, out_shape=(jax.ShapeDtypeStruct(velocity.shape, F3...  38.8 us
    pallas_call x1, Pallas kernels, per_device(): pl.pallas_call(scatter_kernel, grid=(3,), out_shape=(jax.ShapeDtypeStruct...  9.84 us

profile of v5, /device:TPU:1, one launch (start us, length us, event | category | flops | bytes accessed | tf_op | source)
XLA Modules:
  0.0 49.3 jit_solution(12971760250895604783)
XLA Ops:
  0.6 38.8 %shard_map.94 = (f32[3,8,32,512]{3,2,1,0:T(8,128)}, f32[3,32,2048]{2,1,0:T(8,128)}, f32[3,2048]{1,0:T(4,128)}, f32[128,1,128]{2,1,0:T(1,128)}, f32[128,1,128]{2,1,0:T(1,128)}) custom-call(f32[3,8,32,512]{3,2,1,0:T(8,128)} %velocity.1, f32[3,32,2048]{2,1,0:T(8,128)} %bitcast.7, f32[3,2048]{1,0:T(4,128)} %normal_in.1, f32[16,128]{1,0:T(8,128)} %bitcast.10, ...), custom_call_target="tpu_custom_call" | custom-call | tf_op jit(solution)/shard_map/pallas_call | solution.py:558
  39.4 9.8 %shard_map.95 = (f32[3,8,32,512]{3,2,1,0:T(8,128)}, f32[3,32,2048]{2,1,0:T(8,128)}, f32[3,2048]{1,0:T(4,128)}) custom-call(f32[128,128]{1,0:T(8,128)} %bitcast.8, f32[128,128]{1,0:T(8,128)} %bitcast.9, f32[3,8,32,512]{3,2,1,0:T(8,128)} %get-tuple-element.13.base, f32[3,32,2048]{2,1,0:T(8,128)} %get-tuple-element.14.wall_in, ...), custom_call_target="tpu_custom_call" | custom-call | tf_op jit(solution)/shard_map/pallas_call | solution.py:599
